TPU v7x, 32 devices: a whole 2x2x4 slice. The times are simulated.
32 devices in a mesh: task: 4 (over y, x), batch: 8 (over z, core).
Axes of the slice: x: 2, y: 2, z: 4, core: 2. Of those that a mesh axis runs over, the one named last changes fastest.
Arguments:
- tokens: bfloat16 [32768, 1024], P(('task', 'batch')), may hold values from -6 to 6
- lengths: int32 [32, 4], P(('task', 'batch')), may hold values from 0 to 1024, as said below
- task_ids: int32 [32, 4], replicated, may hold values from 0 to 63, as said below
- prefix_embed: bfloat16 [64, 10, 1024], P('task', None, 'batch'), may hold values from -6 to 6
- reparam_inner: bfloat16 [64, 1024, 512], P('task', 'batch'), may hold values from -0.1875 to 0.1875
- reparam_inner_bias: bfloat16 [64, 512], P('task'), may hold values from -3 to 3
- reparam_outer: bfloat16 [64, 512, 2048], P('task', None, 'batch'), may hold values from -0.4375 to 0.4375
- reparam_outer_bias: bfloat16 [64, 2048], P('task', 'batch'), may hold values from -3 to 3
- first_gain: bfloat16 [1024], replicated, may hold values from 0.5 to 1.5
- first_bias: bfloat16 [1024], replicated, may hold values from -3 to 3
- input_weight: bfloat16 [1024, 3072], replicated, may hold values from -0.1875 to 0.1875
- output_weight: bfloat16 [1024, 1024], replicated, may hold values from -1.5 to 1.5
- second_gain: bfloat16 [1024], replicated, may hold values from 0.5 to 1.5
- second_bias: bfloat16 [1024], replicated, may hold values from -3 to 3
- expand_weight: bfloat16 [1024, 4096], replicated, may hold values from -0.1875 to 0.1875
- contract_weight: bfloat16 [4096, 1024], replicated, may hold values from -0.09375 to 0.09375
- output_cotangent: bfloat16 [32768, 1024], P(('task', 'batch')), may hold values from -6 to 6
Outputs:
- output: bfloat16 [32768, 1024], P(('task', 'batch'))
- input_grad: bfloat16 [32768, 1024], P(('task', 'batch'))
- grad_embed: float32 [64, 10, 1024], P('task', None, 'batch')
- grad_inner: float32 [64, 1024, 512], P('task', 'batch')
- grad_inner_bias: float32 [64, 512], P('task')
- grad_outer: float32 [64, 512, 2048], P('task', None, 'batch')
- grad_outer_bias: float32 [64, 2048], P('task', 'batch')
Inputs may be any that keep to these rules, and one draw needn't show every extreme that they name: `task_ids`: the 4 examples of one device have tasks t with 4 different values of t // 16. Each device's row is either 1024 followed by zeros (one sequence) or 4 lengths of 256; both kinds occur in every draw.
All inputs are finite; a program needn't handle non-finite values.
Results may differ from a plain program's by a relative error of at most 0.013.
Values may be sent and summed in bfloat16 or wider, within the bound.
A program may use at most 256 MiB of HBM per device.

v0:
```python
import functools

import jax
import jax.numpy as jnp
from jax import lax
from jax.experimental import pallas as pl
from jax.experimental.pallas import tpu as pltpu
from jax.sharding import PartitionSpec as P

BF = jnp.bfloat16
F = jnp.float32
PAD = 16
NEG = -1e30
MESH = pl.DeviceIdType.MESH


def dg(a, b, ca, cb):
    return lax.dot_general(a, b, (((ca,), (cb,)), ((), ())), preferred_element_type=F)


def attn_fwd_kernel(slots, plen, len_ref, q_ref, k_ref, v_ref, pk_ref, pv_ref, o_ref, lse_ref, km):
    rows, pair = q_ref.shape
    blk = rows // slots
    hd = pair // 2
    scale = hd ** -0.5
    single = len_ref[0, 0] > blk
    first = lax.broadcasted_iota(jnp.int32, (1, pair), 1) < hd
    zero = jnp.zeros((), BF)
    k = k_ref[...]
    km[0] = jnp.where(first, k, zero)
    km[1] = jnp.where(first, zero, k)
    vt = v_ref[...].T
    tri = lax.broadcasted_iota(jnp.int32, (blk, blk), 0) <= lax.broadcasted_iota(jnp.int32, (blk, blk), 1)
    live = lax.broadcasted_iota(jnp.int32, (PAD, blk), 0) < plen
    for i in range(slots):
        lo, hi = i * blk, (i + 1) * blk
        q = q_ref[lo:hi, :] * jnp.asarray(scale, BF)
        kp = jnp.where(single, pk_ref[0:PAD, :], pk_ref[i * PAD:(i + 1) * PAD, :])
        vp = jnp.where(single, pv_ref[0:PAD, :], pv_ref[i * PAD:(i + 1) * PAD, :])
        vpt = jnp.concatenate([jnp.where(first, vp, zero), jnp.where(first, zero, vp)], axis=0).T
        sp = dg(jnp.concatenate([jnp.where(first, kp, zero), jnp.where(first, zero, kp)], axis=0), q, 1, 1)
        outs, tops, sums, pps = [], [], [], []
        for h in range(2):
            s_pre = jnp.where(live, sp[h * PAD:(h + 1) * PAD], NEG)
            s_dia = jnp.where(tri, dg(km[h, lo:hi, :], q, 1, 1), NEG)
            top = jnp.maximum(jnp.max(s_dia, axis=0, keepdims=True), jnp.max(s_pre, axis=0, keepdims=True))
            if i:
                s_off = dg(km[h, 0:lo, :], q, 1, 1)
                top = jnp.maximum(top, jnp.where(single, jnp.max(s_off, axis=0, keepdims=True), NEG))
            p_pre = jnp.exp(s_pre - top)
            p_dia = jnp.exp(s_dia - top)
            total = jnp.sum(p_dia, axis=0, keepdims=True) + jnp.sum(p_pre, axis=0, keepdims=True)
            ot = dg(vt[h * hd:(h + 1) * hd, lo:hi], p_dia.astype(BF), 1, 0)
            if i:
                p_off = jnp.exp(s_off - jnp.where(single, top, -NEG))
                total = total + jnp.sum(p_off, axis=0, keepdims=True)
                ot = ot + dg(vt[h * hd:(h + 1) * hd, 0:lo], p_off.astype(BF), 1, 0)
            outs.append(ot)
            tops.append(top)
            sums.append(total)
            pps.append(p_pre.astype(BF))
        pre = dg(vpt, jnp.concatenate(pps, axis=0), 1, 0)
        for h in range(2):
            outs[h] = (outs[h] + pre[h * hd:(h + 1) * hd]) / sums[h]
            lse_ref[0, h:h + 1, lo:hi] = tops[h] + jnp.log(sums[h])
        o_ref[lo:hi, :] = jnp.concatenate(outs, axis=0).T.astype(BF)


def attn_fwd(lengths, qkv, pkv, plen):
    rows = qkv.shape[0]
    width = qkv.shape[1] // 3
    slots = lengths.shape[1]
    pairs = width // 128
    col = lambda off: pl.BlockSpec((rows, 128), lambda h: (0, h + off))
    pcol = lambda off: pl.BlockSpec((slots * PAD, 128), lambda h: (0, h + off))
    return pl.pallas_call(
        functools.partial(attn_fwd_kernel, slots, plen),
        grid=(pairs,),
        in_specs=[pl.BlockSpec(memory_space=pltpu.SMEM), col(0), col(pairs), col(2 * pairs), pcol(0), pcol(pairs)],
        out_specs=[col(0), pl.BlockSpec((1, 2, rows), lambda h: (h, 0, 0))],
        out_shape=[jax.ShapeDtypeStruct((rows, width), BF), jax.ShapeDtypeStruct((pairs, 2, rows), F)],
        scratch_shapes=[pltpu.VMEM((2, rows, 128), BF)],
        compiler_params=pltpu.CompilerParams(vmem_limit_bytes=62 * 2**20),
        name="attend",
    )(lengths, qkv, qkv, qkv, pkv, pkv)


def attn_bwd_kernel(slots, plen, len_ref, q_ref, k_ref, v_ref, pk_ref, pv_ref, o_ref, do_ref, lse_ref,
                    dq_ref, dk_ref, dv_ref, dpk_ref, dpv_ref, km, vm, dka, dva):
    rows, pair = q_ref.shape
    blk = rows // slots
    hd = pair // 2
    scale = hd ** -0.5
    single = len_ref[0, 0] > blk
    first = lax.broadcasted_iota(jnp.int32, (1, pair), 1) < hd
    zero = jnp.zeros((), BF)
    split = lambda a: (jnp.where(first, a, zero), jnp.where(first, zero, a))
    stack = lambda a: jnp.concatenate(split(a), axis=0)
    k = k_ref[...]
    km[0], km[1] = split(k)
    vm[0], vm[1] = split(v_ref[...])
    kt = k.T
    tri = lax.broadcasted_iota(jnp.int32, (blk, blk), 0) <= lax.broadcasted_iota(jnp.int32, (blk, blk), 1)
    live = lax.broadcasted_iota(jnp.int32, (PAD, blk), 0) < plen
    pk_sum = pv_sum = None
    pk_parts, pv_parts = [], []
    for i in range(slots):
        lo, hi = i * blk, (i + 1) * blk
        q = q_ref[lo:hi, :] * jnp.asarray(scale, BF)
        do = do_ref[lo:hi, :]
        kp = stack(jnp.where(single, pk_ref[0:PAD, :], pk_ref[i * PAD:(i + 1) * PAD, :]))
        vp = stack(jnp.where(single, pv_ref[0:PAD, :], pv_ref[i * PAD:(i + 1) * PAD, :]))
        sp = dg(kp, q, 1, 1)
        dpp = dg(vp, do, 1, 1)
        prod = (do.astype(F) * o_ref[lo:hi, :].astype(F)).T
        qs = split(q)
        dos = split(do)
        dqs, dsps = [], []
        dk_new = dv_new = None
        add = lambda a, b: b if a is None else a + b
        pkp = pvp = None
        offk = offv = diak = diav = None
        for h in range(2):
            lse = lse_ref[0, h:h + 1, lo:hi]
            delta = jnp.sum(prod[h * hd:(h + 1) * hd], axis=0, keepdims=True)
            p_pre = jnp.where(live, jnp.exp(sp[h * PAD:(h + 1) * PAD] - lse), 0.0)
            ds_pre = (p_pre * (dpp[h * PAD:(h + 1) * PAD] - delta)).astype(BF)
            p_dia = jnp.where(tri, jnp.exp(dg(km[h, lo:hi, :], q, 1, 1) - lse), 0.0)
            ds_dia = (p_dia * (dg(vm[h, lo:hi, :], do, 1, 1) - delta)).astype(BF)
            diav = add(diav, dg(p_dia.astype(BF), dos[h], 1, 0))
            diak = add(diak, dg(ds_dia, qs[h], 1, 0))
            pvp = add(pvp, dg(p_pre.astype(BF), dos[h], 1, 0))
            pkp = add(pkp, dg(ds_pre, qs[h], 1, 0))
            dqt = dg(kt[h * hd:(h + 1) * hd, lo:hi], ds_dia, 1, 0)
            if i:
                p_off = jnp.exp(dg(km[h, 0:lo, :], q, 1, 1) - jnp.where(single, lse, -NEG))
                ds_off = (p_off * (dg(vm[h, 0:lo, :], do, 1, 1) - delta)).astype(BF)
                offv = add(offv, dg(p_off.astype(BF), dos[h], 1, 0))
                offk = add(offk, dg(ds_off, qs[h], 1, 0))
                dqt = dqt + dg(kt[h * hd:(h + 1) * hd, 0:lo], ds_off, 1, 0)
            dqs.append(dqt)
            dsps.append(ds_pre)
        dqt = jnp.concatenate(dqs, axis=0) + dg(kp.T, jnp.concatenate(dsps, axis=0), 1, 0)
        dq_ref[lo:hi, :] = (dqt.T * scale).astype(BF)
        dka[lo:hi, :] = diak
        dva[lo:hi, :] = diav
        if i:
            dka[0:lo, :] += offk
            dva[0:lo, :] += offv
        pk_parts.append(pkp)
        pv_parts.append(pvp)
    dk_ref[...] = dka[...].astype(BF)
    dv_ref[...] = dva[...].astype(BF)
    for i in range(slots):
        for ref, parts in ((dpk_ref, pk_parts), (dpv_ref, pv_parts)):
            whole = sum(parts) if i == 0 else jnp.zeros_like(parts[0])
            ref[i * PAD:(i + 1) * PAD, :] = jnp.where(single, whole, parts[i])


def attn_bwd(lengths, qkv, pkv, attended, grad_att, lse, plen):
    rows = qkv.shape[0]
    width = qkv.shape[1] // 3
    slots = lengths.shape[1]
    pairs = width // 128
    col = lambda off: pl.BlockSpec((rows, 128), lambda h: (0, h + off))
    pcol = lambda off: pl.BlockSpec((slots * PAD, 128), lambda h: (0, h + off))
    sds = jax.ShapeDtypeStruct
    return pl.pallas_call(
        functools.partial(attn_bwd_kernel, slots, plen),
        grid=(pairs,),
        in_specs=[pl.BlockSpec(memory_space=pltpu.SMEM), col(0), col(pairs), col(2 * pairs), pcol(0), pcol(pairs),
                  col(0), col(0), pl.BlockSpec((1, 2, rows), lambda h: (h, 0, 0))],
        out_specs=[col(0), col(0), col(0), pcol(0), pcol(0)],
        out_shape=[sds((rows, width), BF)] * 3 + [sds((slots * PAD, width), F)] * 2,
        scratch_shapes=[pltpu.VMEM((2, rows, 128), BF)] * 2 + [pltpu.VMEM((rows, 128), F)] * 2,
        compiler_params=pltpu.CompilerParams(vmem_limit_bytes=62 * 2**20),
        name="attend_back",
    )(lengths, qkv, qkv, qkv, pkv, pkv, attended, grad_att, lse)


def peer_id(flat, nb):
    return {"task": flat // nb, "batch": flat % nb}


def layer_norm_rows(x, gain, bias):
    inv = 1.0 / x.shape[1]
    mean = jnp.sum(x, axis=1, keepdims=True) * inv
    cen = x - mean
    var = jnp.sum(cen * cen, axis=1, keepdims=True) * inv
    return cen * lax.rsqrt(var + 1e-5) * gain + bias


def greet_all(nt, nb):
    me = lax.axis_index("task") * nb + lax.axis_index("batch")
    total = nt * nb
    barrier = pltpu.get_barrier_semaphore()

    def greet(d, c):
        pl.semaphore_signal(barrier, inc=1, device_id=peer_id(lax.rem(me + d, total), nb), device_id_type=MESH)
        return c

    lax.fori_loop(1, total, greet, 0)
    return barrier, me, total


def front_kernel(nt, nb, td, plen, chunk, cuts,
                 ids_ref, emb_ref, ib_ref, ob_ref, g_ref, b_ref, tok_hbm, w_hbm, inner_hbm, outer_hbm,
                 qkv_hbm, pkv_ref, hid_ref, low_ref,
                 tok, w, inner, outer, normed, qkv, pre, emf, ibf, tbl, rs_out, rs_in, ag_out, ag_in, aa_out, aa_in,
                 ld_sem, st_sem, rs_ss, rs_rs, ag_ss, ag_rs, aa_ss, aa_rs):
    rows, width = tok.shape
    slots = ids_ref.shape[0]
    rc = td * PAD // nb
    pc = outer.shape[2]
    mt = lax.axis_index("task")
    mb = lax.axis_index("batch")
    loads = [pltpu.make_async_copy(s, d, ld_sem.at[i])
             for i, (s, d) in enumerate(((inner_hbm, inner), (tok_hbm, tok), (w_hbm, w), (outer_hbm, outer)))]
    for c in loads:
        c.start()
    barrier, me, total = greet_all(nt, nb)
    pre[...] = jnp.zeros_like(pre)
    emf[...] = emb_ref[...].astype(F).reshape(emf.shape)
    loads[0].wait()
    for t in range(td):
        pre[t * PAD:t * PAD + plen, :] = dg(emf[pl.ds(t, plen, stride=td), :].astype(BF), inner[t], 1, 0)
    for c in range(nb):
        rs_out[c, 0:rc, :] = pre[c * rc:(c + 1) * rc, :].astype(BF)
    ib = ib_ref[...].astype(F)
    for t in range(td):
        ibf[t * PAD:(t + 1) * PAD, :] = jnp.broadcast_to(ib[t:t + 1], (PAD, ib.shape[1]))
    pl.semaphore_wait(barrier, total - 1)

    def batch_copy(d, src, dst, ss, rs):
        to = lax.rem(mb + d, nb)
        return pltpu.make_async_remote_copy(src_ref=src(to), dst_ref=dst, send_sem=ss.at[d], recv_sem=rs.at[d],
                                            device_id={"task": mt, "batch": to}, device_id_type=MESH)

    rs_copy = [batch_copy(d, lambda to: rs_out.at[to], rs_in.at[d], rs_ss, rs_rs) for d in range(1, nb)]
    for c in rs_copy:
        c.start()
    loads[1].wait()
    gain = g_ref[...].astype(F).reshape(1, -1)
    bias = b_ref[...].astype(F).reshape(1, -1)

    def norm_step(i, c):
        r = pl.ds(pl.multiple_of(i * 128, 128), 128)
        normed[r, :] = layer_norm_rows(tok[r, :].astype(F), gain, bias).astype(BF)
        return c

    lax.fori_loop(0, rows // 128, norm_step, 0)
    loads[2].wait()

    def store(j):
        cols = pl.ds(pl.multiple_of(j * chunk, chunk), chunk)
        return pltpu.make_async_copy(qkv.at[:, cols], qkv_hbm.at[:, cols], st_sem.at[j])

    def mm_step(j, c):
        cols = pl.ds(pl.multiple_of(j * chunk, chunk), chunk)
        qkv[:, cols] = dg(normed[...], w[:, cols], 1, 0).astype(BF)
        store(j).start()
        return c

    steps = w.shape[1] // chunk
    c1, c2 = cuts
    lax.fori_loop(0, c1, mm_step, 0)
    mine = pl.ds(pl.multiple_of(mb * rc, rc), rc)
    own = pre[mine, :] + ibf[mine, :]
    for c in rs_copy:
        c.wait_recv()
    for d in range(1, nb):
        own = own + rs_in[d, 0:rc, :].astype(F)
    hid = jnp.tanh(own)
    hid_ref[...] = hid
    ag_out[0:rc, :] = hid.astype(BF)
    ag_copy = [batch_copy(d, lambda to: ag_out, ag_in.at[d], ag_ss, ag_rs) for d in range(1, nb)]
    for c in ag_copy:
        c.start()
    lax.fori_loop(c1, c2, mm_step, 0)

    def put_low(frm, block):
        low_ref[pl.ds(pl.multiple_of(frm * rc, rc), rc), :] = block

    put_low(mb, ag_out[0:rc, :])
    for c in ag_copy:
        c.wait_recv()
    for d in range(1, nb):
        put_low(lax.rem(mb + nb - d, nb), ag_in[d, 0:rc, :])
    loads[3].wait()
    ob = ob_ref[...].astype(F)
    for t in range(td):
        tbl[t] = (dg(low_ref[t * PAD:(t + 1) * PAD, :], outer[t], 1, 0) + ob[t:t + 1]).astype(BF)

    def aa_copy(d):
        to = lax.rem(me + d, total)
        return pltpu.make_async_remote_copy(src_ref=aa_out.at[to], dst_ref=aa_in.at[me], send_sem=aa_ss.at[d],
                                            recv_sem=aa_rs.at[me], device_id=peer_id(to, nb), device_id_type=MESH)

    def pick(e):
        idx = jnp.int32(0)
        for s in range(slots):
            tid = ids_ref[s, e]
            idx = jnp.where(tid // td == mt, lax.rem(tid, td), idx)
        return tbl[idx]

    def aa_step(d, c):
        to = lax.rem(me + d, total)
        aa_out[to] = pick(to)
        aa_copy(d).start()
        return c

    lax.fori_loop(1, total, aa_step, 0)
    aa_in[me] = pick(me)
    lax.fori_loop(c2, steps, mm_step, 0)

    def aa_wait(d, c):
        frm = lax.rem(me + d, total)
        pltpu.make_async_remote_copy(src_ref=aa_out.at[frm], dst_ref=aa_in.at[frm], send_sem=aa_ss.at[d],
                                     recv_sem=aa_rs.at[frm], device_id=peer_id(frm, nb), device_id_type=MESH).wait()
        return c

    lax.fori_loop(1, total, aa_wait, 0)
    for s in range(slots):
        owner = ids_ref[s, me] // td
        for b in range(nb):
            pkv_ref[s * PAD:(s + 1) * PAD, b * pc:(b + 1) * pc] = aa_in[owner * nb + b]
    for c in rs_copy + ag_copy:
        c.wait_send()

    def st_wait(j, c):
        store(j).wait()
        return c

    lax.fori_loop(0, steps, st_wait, 0)


def front(nt, nb, task_ids, prefix_embed, inner, inner_bias, outer, outer_bias, gain, bias, tokens, weight):
    plen, td, depth = prefix_embed.shape
    rep = inner.shape[2]
    pc = outer.shape[2]
    rows, width = tokens.shape
    slots = task_ids.shape[0]
    total = nt * nb
    rc = td * PAD // nb
    rb = max(rc, PAD)
    chunk = 1024
    steps = weight.shape[1] // chunk
    cuts = (steps // 3, 2 * steps // 3)
    sds = jax.ShapeDtypeStruct
    vm = pl.BlockSpec(memory_space=pltpu.VMEM)
    hb = pl.BlockSpec(memory_space=pl.ANY)
    dma = pltpu.SemaphoreType.DMA
    return pl.pallas_call(
        functools.partial(front_kernel, nt, nb, td, plen, chunk, cuts),
        in_specs=[pl.BlockSpec(memory_space=pltpu.SMEM), vm, vm, vm, vm, vm, hb, hb, hb, hb],
        out_specs=[hb, vm, vm, vm],
        out_shape=[sds((rows, weight.shape[1]), BF), sds((slots * PAD, nb * pc), BF), sds((rc, rep), F),
                   sds((td * PAD, rep), BF)],
        scratch_shapes=[
            pltpu.VMEM((rows, width), BF), pltpu.VMEM(weight.shape, BF), pltpu.VMEM(inner.shape, BF),
            pltpu.VMEM(outer.shape, BF), pltpu.VMEM((rows, width), BF), pltpu.VMEM((rows, weight.shape[1]), BF),
            pltpu.VMEM((td * PAD, rep), F), pltpu.VMEM((plen * td, depth), F), pltpu.VMEM((td * PAD, rep), F), pltpu.VMEM((td, PAD, pc), BF),
            pltpu.VMEM((nb, rb, rep), BF), pltpu.VMEM((nb, rb, rep), BF),
            pltpu.VMEM((rb, rep), BF), pltpu.VMEM((nb, rb, rep), BF),
            pltpu.VMEM((total, PAD, pc), BF), pltpu.VMEM((total, PAD, pc), BF),
            dma((4,)), dma((steps,)), dma((nb,)), dma((nb,)), dma((nb,)), dma((nb,)), dma((total,)), dma((total,)),
        ],
        compiler_params=pltpu.CompilerParams(vmem_limit_bytes=62 * 2**20, collective_id=0, has_side_effects=True),
        name="front",
    )(task_ids, prefix_embed, inner_bias, outer_bias, gain, bias,
      tokens, weight, inner, outer)


def middle_kernel(blk, fch, g_ref, b_ref, tok_hbm, att_hbm, ct_hbm, wo_hbm, we_hbm, wc_hbm,
                  out_hbm, gm_hbm, ga_hbm,
                  tok, att, ct, wo, we, wc, mid, n2, mean_s, rstd_s, ld_sem, st_sem):
    rows, width = tok.shape
    ff = we.shape[1]
    names = ((wo_hbm, wo), (att_hbm, att), (tok_hbm, tok), (we_hbm, we), (ct_hbm, ct), (wc_hbm, wc))
    loads = [pltpu.make_async_copy(s, d, ld_sem.at[i]) for i, (s, d) in enumerate(names)]
    for c in loads:
        c.start()
    gain = g_ref[...].astype(F).reshape(1, -1)
    bias = b_ref[...].astype(F).reshape(1, -1)
    inv = 1.0 / width
    steps = rows // blk
    for c in loads[:3]:
        c.wait()

    def first(i, c):
        r = pl.ds(pl.multiple_of(i * blk, blk), blk)
        x = tok[r, :].astype(F) + dg(att[r, :], wo[...], 1, 0)
        mid[r, :] = x
        mean = jnp.sum(x, axis=1, keepdims=True) * inv
        cen = x - mean
        rstd = lax.rsqrt(jnp.sum(cen * cen, axis=1, keepdims=True) * inv + 1e-5)
        mean_s[r, :] = mean
        rstd_s[r, :] = rstd
        n2[r, :] = (cen * rstd * gain + bias).astype(BF)
        return c

    lax.fori_loop(0, steps, first, 0)
    for c in loads[3:]:
        c.wait()

    def stores(i):
        r = pl.ds(pl.multiple_of(i * blk, blk), blk)
        return [pltpu.make_async_copy(s.at[r, :], d.at[r, :], st_sem.at[k, i])
                for k, (s, d) in enumerate(((tok, out_hbm), (mid, gm_hbm), (att, ga_hbm)))]

    def second(i, c):
        r = pl.ds(pl.multiple_of(i * blk, blk), blk)
        x2 = n2[r, :]
        g = ct[r, :]
        pair = lambda k: (dg(x2, we[:, k:k + fch], 1, 0), dg(g, wc[k:k + fch, :], 1, 1))
        y = gn = None
        nxt = pair(0)
        for k in range(0, ff, fch):
            v, up = nxt
            if k + fch < ff:
                nxt = pair(k + fch)
            vv = v * v
            t = jnp.tanh(v * (0.7978845608028654 + (0.7978845608028654 * 0.044715) * vv))
            half = 0.5 + 0.5 * t
            act = (v * half).astype(BF)
            slope = half + v * (0.5 - 0.5 * t * t) * (0.7978845608028654 + (3 * 0.7978845608028654 * 0.044715) * vv)
            gh = (up * slope).astype(BF)
            yk = dg(act, wc[k:k + fch, :], 1, 0)
            gk = dg(gh, we[:, k:k + fch], 1, 1)
            y = yk if y is None else y + yk
            gn = gk if gn is None else gn + gk
        x = mid[r, :]
        tok[r, :] = (x + y).astype(BF)
        rstd = rstd_s[r, :]
        xhat = (x - mean_s[r, :]) * rstd
        ug = gn * gain
        m1 = jnp.sum(ug, axis=1, keepdims=True) * inv
        m2 = jnp.sum(ug * xhat, axis=1, keepdims=True) * inv
        gmid = g.astype(F) + rstd * (ug - m1 - xhat * m2)
        mid[r, :] = gmid
        att[r, :] = dg(gmid.astype(BF), wo[...], 1, 1).astype(BF)
        for cp in stores(i):
            cp.start()
        return c

    lax.fori_loop(0, steps, second, 0)
    for i in range(steps):
        for cp in stores(i):
            cp.wait()


def middle(gain, bias, tokens, attended, ct, wo, we, wc, blk=256, fch=512):
    rows, width = tokens.shape
    ff = we.shape[1]
    sds = jax.ShapeDtypeStruct
    vm = pl.BlockSpec(memory_space=pltpu.VMEM)
    hb = pl.BlockSpec(memory_space=pl.ANY)
    dma = pltpu.SemaphoreType.DMA
    full = lambda t: pltpu.VMEM((rows, width), t)
    return pl.pallas_call(
        functools.partial(middle_kernel, blk, fch),
        in_specs=[vm, vm] + [hb] * 6,
        out_specs=[hb] * 3,
        out_shape=[sds((rows, width), BF), sds((rows, width), F), sds((rows, width), BF)],
        scratch_shapes=[full(BF), full(BF), full(BF), pltpu.VMEM(wo.shape, BF), pltpu.VMEM(we.shape, BF),
                        pltpu.VMEM(wc.shape, BF), full(F), full(BF), pltpu.VMEM((rows, 1), F), pltpu.VMEM((rows, 1), F),
                        dma((6,)), dma((3, rows // blk))],
        compiler_params=pltpu.CompilerParams(vmem_limit_bytes=62 * 2**20),
        name="middle",
    )(gain, bias, tokens, attended, ct, wo, we, wc)


def back_kernel(nt, nb, td, blk,
                ids_ref, hid_ref, g_ref, dpk_ref, dpv_ref, outer_hbm, w_hbm, dq_hbm, dk_hbm, dv_hbm, tok_hbm, gm_hbm,
                ig_hbm, gpre_ref, gtl_ref,
                outer, w, dq, dk, dv, tok, gm, ig, sel, rs_out, rs_in, ag_out, ag_in, aa_out, aa_in, part,
                ld_sem, st_sem, rs_ss, rs_rs, ag_ss, ag_rs, aa_ss, aa_rs):
    rows, width = tok.shape
    slots = ids_ref.shape[0]
    rc = td * PAD // nb
    pc = outer.shape[2]
    mt = lax.axis_index("task")
    mb = lax.axis_index("batch")
    names = ((w_hbm, w), (dq_hbm, dq), (dk_hbm, dk), (dv_hbm, dv), (tok_hbm, tok), (gm_hbm, gm), (outer_hbm, outer))
    loads = [pltpu.make_async_copy(s, d, ld_sem.at[i]) for i, (s, d) in enumerate(names)]
    for c in loads:
        c.start()
    barrier, me, total = greet_all(nt, nb)
    for o in range(nt):
        at = jnp.int32(0)
        for s in range(slots):
            at = jnp.where(ids_ref[s, me] // td == o, s, at)
        for half, ref in enumerate((dpk_ref, dpv_ref)):
            block = ref[at].astype(BF)
            for b in range(nb // 2):
                aa_out[o * nb + half * (nb // 2) + b] = block[:, b * pc:(b + 1) * pc]
    pl.semaphore_wait(barrier, total - 1)

    def aa_copy(d, to, at):
        return pltpu.make_async_remote_copy(src_ref=aa_out.at[to], dst_ref=aa_in.at[at], send_sem=aa_ss.at[d],
                                            recv_sem=aa_rs.at[at], device_id=peer_id(to, nb), device_id_type=MESH)

    def aa_step(d, c):
        aa_copy(d, lax.rem(me + d, total), me).start()
        return c

    lax.fori_loop(1, total, aa_step, 0)
    aa_in[me] = aa_out[me]
    lane = lax.broadcasted_iota(jnp.int32, (1, total * PAD), 1)
    task_of = jnp.zeros((1, total * PAD), jnp.int32)
    for e in range(total):
        idx = jnp.int32(0)
        for s in range(slots):
            tid = ids_ref[s, e]
            idx = jnp.where(tid // td == mt, lax.rem(tid, td), idx)
        task_of = jnp.where(lane // PAD == e, idx, task_of)
    want = task_of * PAD + lax.rem(lane, PAD)
    row = lax.broadcasted_iota(jnp.int32, (td * PAD, total * PAD), 0)
    sel[...] = jnp.where(row == want, 1.0, 0.0).astype(BF)
    gain = g_ref[...].astype(F).reshape(1, -1)
    for c in loads[:6]:
        c.wait()
    inv = 1.0 / width

    def store(i):
        r = pl.ds(pl.multiple_of(i * blk, blk), blk)
        return pltpu.make_async_copy(ig.at[r, :], ig_hbm.at[r, :], st_sem.at[i])

    def mm_step(i, c):
        r = pl.ds(pl.multiple_of(i * blk, blk), blk)
        gn = (dg(dq[r, :], w[:, 0:width], 1, 1) + dg(dk[r, :], w[:, width:2 * width], 1, 1)
              + dg(dv[r, :], w[:, 2 * width:], 1, 1))
        ug = gn * gain
        x = tok[r, :].astype(F)
        cen = x - jnp.sum(x, axis=1, keepdims=True) * inv
        rstd = lax.rsqrt(jnp.sum(cen * cen, axis=1, keepdims=True) * inv + 1e-5)
        xhat = cen * rstd
        m1 = jnp.sum(ug, axis=1, keepdims=True) * inv
        m2 = jnp.sum(ug * xhat, axis=1, keepdims=True) * inv
        ig[r, :] = (gm[r, :] + rstd * (ug - m1 - xhat * m2)).astype(BF)
        store(i).start()
        return c

    steps = rows // blk
    c1, c2 = steps // 4, 3 * steps // 4
    lax.fori_loop(0, c1, mm_step, 0)

    def aa_wait(d, c):
        frm = lax.rem(me + d, total)
        aa_copy(d, frm, frm).wait()
        return c

    lax.fori_loop(1, total, aa_wait, 0)
    gtl_ref[...] = dg(sel[...], aa_in[...].reshape(total * PAD, pc), 1, 0).astype(BF)
    loads[6].wait()
    for t in range(td):
        part[t * PAD:(t + 1) * PAD, :] = dg(gtl_ref[t * PAD:(t + 1) * PAD, :], outer[t], 1, 1)
    for c in range(nb):
        rs_out[c, 0:rc, :] = part[c * rc:(c + 1) * rc, :].astype(BF)

    def batch_copy(d, src, dst, ss, rs):
        to = lax.rem(mb + d, nb)
        return pltpu.make_async_remote_copy(src_ref=src(to), dst_ref=dst, send_sem=ss.at[d], recv_sem=rs.at[d],
                                            device_id={"task": mt, "batch": to}, device_id_type=MESH)

    rs_copy = [batch_copy(d, lambda to: rs_out.at[to], rs_in.at[d], rs_ss, rs_rs) for d in range(1, nb)]
    for c in rs_copy:
        c.start()
    lax.fori_loop(c1, c2, mm_step, 0)
    own = part[pl.ds(pl.multiple_of(mb * rc, rc), rc), :]
    for c in rs_copy:
        c.wait_recv()
    for d in range(1, nb):
        own = own + rs_in[d, 0:rc, :].astype(F)
    hid = hid_ref[...]
    ag_out[0:rc, :] = (own * (1.0 - hid * hid)).astype(BF)
    ag_copy = [batch_copy(d, lambda to: ag_out, ag_in.at[d], ag_ss, ag_rs) for d in range(1, nb)]
    for c in ag_copy:
        c.start()
    lax.fori_loop(c2, steps, mm_step, 0)

    def put(frm, block):
        gpre_ref[pl.ds(pl.multiple_of(frm * rc, rc), rc), :] = block

    put(mb, ag_out[0:rc, :])
    for c in ag_copy:
        c.wait_recv()
    for d in range(1, nb):
        put(lax.rem(mb + nb - d, nb), ag_in[d, 0:rc, :])
    for c in rs_copy + ag_copy:
        c.wait_send()
    for i in range(steps):
        store(i).wait()


def back(nt, nb, task_ids, hid, gain, dpk, dpv, outer, weight, dq, dk, dv, tokens, grad_mid):
    td, rep, pc = outer.shape
    rows, width = tokens.shape
    slots = task_ids.shape[0]
    total = nt * nb
    rc = td * PAD // nb
    rb = max(rc, PAD)
    blk = 256
    sds = jax.ShapeDtypeStruct
    vm = pl.BlockSpec(memory_space=pltpu.VMEM)
    hb = pl.BlockSpec(memory_space=pl.ANY)
    dma = pltpu.SemaphoreType.DMA
    return pl.pallas_call(
        functools.partial(back_kernel, nt, nb, td, blk),
        in_specs=[pl.BlockSpec(memory_space=pltpu.SMEM), vm, vm, vm, vm] + [hb] * 7,
        out_specs=[hb, vm, vm],
        out_shape=[sds((rows, width), BF), sds((td * PAD, rep), BF), sds((td * PAD, pc), BF)],
        scratch_shapes=[
            pltpu.VMEM(outer.shape, BF), pltpu.VMEM(weight.shape, BF)] + [pltpu.VMEM((rows, width), BF)] * 4 + [
            pltpu.VMEM((rows, width), F), pltpu.VMEM((rows, width), BF),
            pltpu.VMEM((td * PAD, total * PAD), BF),
            pltpu.VMEM((nb, rb, rep), BF), pltpu.VMEM((nb, rb, rep), BF),
            pltpu.VMEM((rb, rep), BF), pltpu.VMEM((nb, rb, rep), BF),
            pltpu.VMEM((total, PAD, pc), BF), pltpu.VMEM((total, PAD, pc), BF),
            pltpu.VMEM((td * PAD, rep), F),
            dma((7,)), dma((rows // blk,)), dma((nb,)), dma((nb,)), dma((nb,)), dma((nb,)), dma((total,)), dma((total,)),
        ],
        compiler_params=pltpu.CompilerParams(vmem_limit_bytes=62 * 2**20, collective_id=1, has_side_effects=True),
        name="back",
    )(task_ids, hid, gain, dpk.reshape(slots, PAD, width), dpv.reshape(slots, PAD, width),
      outer, weight, dq, dk, dv, tokens, grad_mid)


def tail_kernel(plen, ig_in, emb_ref, inner_ref, gpre_ref, low_ref, gtl_ref,
                ig_out, ge_ref, gi_ref, gib_ref, go_ref, gob_ref, emf):
    step = pl.program_id(0)
    ig_out[...] = ig_in[...]

    @pl.when(step == 0)
    def _():
        emf[...] = emb_ref[...].astype(F).reshape(emf.shape)

    per = inner_ref.shape[0]
    td = gib_ref.shape[0]
    for k in range(per):
        r = slice(k * PAD, (k + 1) * PAD)
        gp = gpre_ref[r, :]
        gt = gtl_ref[r, :]
        at = pl.ds(step * per + k, 1)
        spread = pl.ds(step * per + k, plen, stride=td)
        gi_ref[k] = dg(emf[spread, :].astype(BF), gp[0:plen], 0, 0)
        go_ref[k] = dg(low_ref[r, :], gt, 0, 0)
        ge_ref[spread, :] = dg(gp, inner_ref[k], 1, 1)[0:plen]
        gib_ref[at, :] = jnp.sum(gp[0:plen].astype(F), axis=0, keepdims=True)
        gob_ref[at, :] = jnp.sum(gt[0:plen].astype(F), axis=0, keepdims=True)


def tail(ig, emb, inner, gpre, low, gtl):
    plen, td, depth = emb.shape
    rep = inner.shape[2]
    pc = gtl.shape[1]
    per = 2
    sds = jax.ShapeDtypeStruct
    rows = pl.BlockSpec((ig.shape[0] * per // td, ig.shape[1]), lambda i: (i, 0))
    lead = lambda *shape: pl.BlockSpec((per,) + shape, lambda i: (i,) + (0,) * len(shape))
    flat = lambda cols: pl.BlockSpec((per * PAD, cols), lambda i: (i, 0))
    full = lambda cols: pl.BlockSpec((td, cols), lambda i: (0, 0))
    return pl.pallas_call(
        functools.partial(tail_kernel, plen),
        grid=(td // per,),
        in_specs=[rows, pl.BlockSpec((plen, td, depth), lambda i: (0, 0, 0)), lead(depth, rep), flat(rep), flat(rep), flat(pc)],
        out_specs=[rows, pl.BlockSpec((plen * td, depth), lambda i: (0, 0)), lead(depth, rep), full(rep), lead(rep, pc), full(pc)],
        out_shape=[sds(ig.shape, BF), sds((plen * td, depth), F), sds((td, depth, rep), F), sds((td, rep), F),
                   sds((td, rep, pc), F), sds((td, pc), F)],
        scratch_shapes=[pltpu.VMEM((plen * td, depth), F)],
        compiler_params=pltpu.CompilerParams(vmem_limit_bytes=62 * 2**20),
        name="tail",
    )(ig, emb, inner, gpre, low, gtl)


def local(
    tokens,
    lengths,
    task_ids,
    prefix_embed,
    reparam_inner,
    reparam_inner_bias,
    reparam_outer,
    reparam_outer_bias,
    first_gain,
    first_bias,
    input_weight,
    output_weight,
    second_gain,
    second_bias,
    expand_weight,
    contract_weight,
    output_cotangent,
):
    prefix_len = prefix_embed.shape[1]
    task_count = lax.axis_size("task")
    batch_count = lax.axis_size("batch")
    ids = task_ids.T
    embed = prefix_embed.transpose(1, 0, 2)
    projected, prefix_kv, hidden_chunk, hidden_low = front(
        task_count, batch_count, ids, embed, reparam_inner, reparam_inner_bias, reparam_outer,
        reparam_outer_bias, first_gain, first_bias, tokens, input_weight,
    )
    attended, log_totals = attn_fwd(lengths, projected, prefix_kv, prefix_len)
    output, grad_mid, grad_attended = middle(
        second_gain, second_bias, tokens, attended, output_cotangent, output_weight, expand_weight, contract_weight
    )
    grad_q, grad_k, grad_v, grad_pk, grad_pv = attn_bwd(
        lengths, projected, prefix_kv, attended, grad_attended, log_totals, prefix_len
    )
    input_grad, grad_pre, grad_table = back(
        task_count, batch_count, ids, hidden_chunk, first_gain, grad_pk, grad_pv, reparam_outer, input_weight,
        grad_q, grad_k, grad_v, tokens, grad_mid,
    )
    input_grad, grad_embed, grad_inner, grad_inner_bias, grad_outer, grad_outer_bias = tail(
        input_grad, embed, reparam_inner, grad_pre, hidden_low, grad_table
    )
    grad_embed = grad_embed.reshape(embed.shape).transpose(1, 0, 2)
    return (
        output,
        input_grad,
        grad_embed,
        grad_inner,
        grad_inner_bias,
        grad_outer,
        grad_outer_bias,
    )


def solution(mesh):
    placed = (
        P(("task", "batch"), None),
        P(("task", "batch"), None),
        P(),
        P("task", None, "batch"),
        P("task", "batch", None),
        P("task", None),
        P("task", None, "batch"),
        P("task", "batch"),
        P(),
        P(),
        P(),
        P(),
        P(),
        P(),
        P(),
        P(),
        P(("task", "batch"), None),
    )
    return jax.shard_map(
        local,
        mesh=mesh,
        in_specs=placed,
        out_specs=(
            P(("task", "batch"), None),
            P(("task", "batch"), None),
            P("task", None, "batch"),
            P("task", "batch", None),
            P("task", None),
            P("task", None, "batch"),
            P("task", "batch"),
        ),
        check_vma=False,
    )
```

profile of v0, /device:TPU:0, one launch (start us, length us, event | category | flops | bytes accessed | tf_op | source)
XLA Modules:
  0.0 187.0 jit_solution(18212878862776714780)
XLA Ops:
  0.6 31.6 %front.1 = (bf16[1024,3072]{1,0:T(8,128)(2,1)}, bf16[64,2048]{1,0:T(8,128)(2,1)}, f32[32,512]{1,0:T(8,128)}, bf16[256,512]{1,0:T(8,128)(2,1)}) custom-call(s32[4,32]{1,0:T(4,128)} %bitcast.11, bf16[10,16,128]{2,1,0:T(8,128)(2,1)} %bitcast.9, bf16[16,512]{1,0:T(8,128)(2,1)} %ib_ref.1, bf16[16,256]{1,0:T(8,128)(2,1)} %ob_ref.1, bf16[1024]{0:T(1024)(128)(2,1)} %g_ref.5, ...), custom_call_target="tpu_custom_call" | custom-call | tf_op jit(solution)/shard_map/front/pallas_call | solution.py:353
  32.2 29.6 %attend.1 = (bf16[1024,1024]{1,0:T(8,128)(2,1)}, f32[8,2,1024]{2,1,0:T(2,128)}) custom-call(s32[1,4]{1,0:T(1,128)} %len_ref.3, bf16[1024,3072]{1,0:T(8,128)(2,1)} %get-tuple-element.30.q_ref.k_ref.v_ref, bf16[1024,3072]{1,0:T(8,128)(2,1)} %get-tuple-element.30.q_ref.k_ref.v_ref, bf16[1024,3072]{1,0:T(8,128)(2,1)} %get-tuple-element.30.q_ref.k_ref.v_ref, ...), custom_call_target="tpu_custom_call" | custom-call | tf_op jit(solution)/shard_map/attend/pallas_call | solution.py:76
  61.8 49.9 %middle.1 = (bf16[1024,1024]{1,0:T(8,128)(2,1)}, f32[1024,1024]{1,0:T(8,128)}, bf16[1024,1024]{1,0:T(8,128)(2,1)}) custom-call(bf16[1024]{0:T(1024)(128)(2,1)} %g_ref.4, bf16[1024]{0:T(1024)(128)(2,1)} %b_ref.3, bf16[1024,1024]{1,0:T(8,128)(2,1)} %tok_hbm.5, bf16[1024,1024]{1,0:T(8,128)(2,1)} %get-tuple-element.32.att_hbm.o_ref, bf16[1024,1024]{1,0:T(8,128)(2,1)} %ct_hbm.1, ...), custom_call_target="tpu_custom_call" | custom-call | tf_op jit(solution)/shard_map/middle/pallas_call | solution.py:460
  111.7 37.8 %attend_back.1 = (bf16[1024,1024]{1,0:T(8,128)(2,1)}, bf16[1024,1024]{1,0:T(8,128)(2,1)}, bf16[1024,1024]{1,0:T(8,128)(2,1)}, f32[64,1024]{1,0:T(8,128)}, f32[64,1024]{1,0:T(8,128)}) custom-call(s32[1,4]{1,0:T(1,128)} %len_ref.3, bf16[1024,3072]{1,0:T(8,128)(2,1)} %get-tuple-element.30.q_ref.k_ref.v_ref, ...), custom_call_target="tpu_custom_call" | custom-call | tf_op jit(solution)/shard_map/attend_back/pallas_call | solution.py:168
  149.5 27.8 %back.1 = (bf16[1024,1024]{1,0:T(8,128)(2,1)}, bf16[256,512]{1,0:T(8,128)(2,1)}, bf16[256,256]{1,0:T(8,128)(2,1)}) custom-call(s32[4,32]{1,0:T(4,128)} %bitcast.12, f32[32,512]{1,0:T(8,128)} %get-tuple-element.34.hid_ref, bf16[1024]{0:T(1024)(128)(2,1)} %g_ref.5, f32[4,16,1024]{2,1,0:T(8,128)} %bitcast.7, f32[4,16,1024]{2,1,0:T(8,128)} %bitcast.8, ...), custom_call_target="tpu_custom_call" | custom-call | tf_op jit(solution)/shard_map/back/pallas_call | solution.py:608
  177.3 9.7 %tail.1 = (bf16[1024,1024]{1,0:T(8,128)(2,1)}, f32[160,128]{1,0:T(8,128)}, f32[16,128,512]{2,1,0:T(8,128)}, f32[16,512]{1,0:T(8,128)}, f32[16,512,256]{2,1,0:T(8,128)}, /*index=5*/f32[16,256]{1,0:T(8,128)}) custom-call(bf16[1024,1024]{1,0:T(8,128)(2,1)} %get-tuple-element.43.ig_in, bf16[10,16,128]{2,1,0:T(8,128)(2,1)} %bitcast.10, ...), custom_call_target="tpu_custom_call" | custom-call | tf_op jit(solution)/shard_map/tail/pallas_call | solution.py:663
where the time goes:
time: 188 us; the launch traced here: 187 us
  Pallas kernels  186 us (99%)
    pallas_call x1, Pallas kernels, middle(): pl.pallas_call(functools.partial(middle_kernel, blk, fch), in_specs=[vm,...  49.9 us
    pallas_call x1, Pallas kernels, attn_bwd(): pl.pallas_call(functools.partial(attn_bwd_kernel, slots, plen), grid=(pai...  37.8 us
    pallas_call x1, Pallas kernels, front(): pl.pallas_call(functools.partial(front_kernel, nt, nb, td, plen, chunk, c...  31.6 us
    pallas_call x1, Pallas kernels, attn_fwd(): pl.pallas_call(functools.partial(attn_fwd_kernel, slots, plen), grid=(pai...  29.6 us
    pallas_call x1, Pallas kernels, back(): pl.pallas_call(functools.partial(back_kernel, nt, nb, td, blk), in_specs=...  27.8 us
    pallas_call x1, Pallas kernels, tail(): pl.pallas_call(functools.partial(tail_kernel, plen), grid=(td // per,), i...  9.71 us

commit v1 on v0

--- a/solution.py
+++ b/solution.py
@@ -16,73 +16,6 @@
 
 def dg(a, b, ca, cb):
     return lax.dot_general(a, b, (((ca,), (cb,)), ((), ())), preferred_element_type=F)
-
-
-def attn_fwd_kernel(slots, plen, len_ref, q_ref, k_ref, v_ref, pk_ref, pv_ref, o_ref, lse_ref, km):
-    rows, pair = q_ref.shape
-    blk = rows // slots
-    hd = pair // 2
-    scale = hd ** -0.5
-    single = len_ref[0, 0] > blk
-    first = lax.broadcasted_iota(jnp.int32, (1, pair), 1) < hd
-    zero = jnp.zeros((), BF)
-    k = k_ref[...]
-    km[0] = jnp.where(first, k, zero)
-    km[1] = jnp.where(first, zero, k)
-    vt = v_ref[...].T
-    tri = lax.broadcasted_iota(jnp.int32, (blk, blk), 0) <= lax.broadcasted_iota(jnp.int32, (blk, blk), 1)
-    live = lax.broadcasted_iota(jnp.int32, (PAD, blk), 0) < plen
-    for i in range(slots):
-        lo, hi = i * blk, (i + 1) * blk
-        q = q_ref[lo:hi, :] * jnp.asarray(scale, BF)
-        kp = jnp.where(single, pk_ref[0:PAD, :], pk_ref[i * PAD:(i + 1) * PAD, :])
-        vp = jnp.where(single, pv_ref[0:PAD, :], pv_ref[i * PAD:(i + 1) * PAD, :])
-        vpt = jnp.concatenate([jnp.where(first, vp, zero), jnp.where(first, zero, vp)], axis=0).T
-        sp = dg(jnp.concatenate([jnp.where(first, kp, zero), jnp.where(first, zero, kp)], axis=0), q, 1, 1)
-        outs, tops, sums, pps = [], [], [], []
-        for h in range(2):
-            s_pre = jnp.where(live, sp[h * PAD:(h + 1) * PAD], NEG)
-            s_dia = jnp.where(tri, dg(km[h, lo:hi, :], q, 1, 1), NEG)
-            top = jnp.maximum(jnp.max(s_dia, axis=0, keepdims=True), jnp.max(s_pre, axis=0, keepdims=True))
-            if i:
-                s_off = dg(km[h, 0:lo, :], q, 1, 1)
-                top = jnp.maximum(top, jnp.where(single, jnp.max(s_off, axis=0, keepdims=True), NEG))
-            p_pre = jnp.exp(s_pre - top)
-            p_dia = jnp.exp(s_dia - top)
-            total = jnp.sum(p_dia, axis=0, keepdims=True) + jnp.sum(p_pre, axis=0, keepdims=True)
-            ot = dg(vt[h * hd:(h + 1) * hd, lo:hi], p_dia.astype(BF), 1, 0)
-            if i:
-                p_off = jnp.exp(s_off - jnp.where(single, top, -NEG))
-                total = total + jnp.sum(p_off, axis=0, keepdims=True)
-                ot = ot + dg(vt[h * hd:(h + 1) * hd, 0:lo], p_off.astype(BF), 1, 0)
-            outs.append(ot)
-            tops.append(top)
-            sums.append(total)
-            pps.append(p_pre.astype(BF))
-        pre = dg(vpt, jnp.concatenate(pps, axis=0), 1, 0)
-        for h in range(2):
-            outs[h] = (outs[h] + pre[h * hd:(h + 1) * hd]) / sums[h]
-            lse_ref[0, h:h + 1, lo:hi] = tops[h] + jnp.log(sums[h])
-        o_ref[lo:hi, :] = jnp.concatenate(outs, axis=0).T.astype(BF)
-
-
-def attn_fwd(lengths, qkv, pkv, plen):
-    rows = qkv.shape[0]
-    width = qkv.shape[1] // 3
-    slots = lengths.shape[1]
-    pairs = width // 128
-    col = lambda off: pl.BlockSpec((rows, 128), lambda h: (0, h + off))
-    pcol = lambda off: pl.BlockSpec((slots * PAD, 128), lambda h: (0, h + off))
-    return pl.pallas_call(
-        functools.partial(attn_fwd_kernel, slots, plen),
-        grid=(pairs,),
-        in_specs=[pl.BlockSpec(memory_space=pltpu.SMEM), col(0), col(pairs), col(2 * pairs), pcol(0), pcol(pairs)],
-        out_specs=[col(0), pl.BlockSpec((1, 2, rows), lambda h: (h, 0, 0))],
-        out_shape=[jax.ShapeDtypeStruct((rows, width), BF), jax.ShapeDtypeStruct((pairs, 2, rows), F)],
-        scratch_shapes=[pltpu.VMEM((2, rows, 128), BF)],
-        compiler_params=pltpu.CompilerParams(vmem_limit_bytes=62 * 2**20),
-        name="attend",
-    )(lengths, qkv, qkv, qkv, pkv, pkv)
 
 
 def attn_bwd_kernel(slots, plen, len_ref, q_ref, k_ref, v_ref, pk_ref, pv_ref, o_ref, do_ref, lse_ref,
@@ -102,53 +35,76 @@
     kt = k.T
     tri = lax.broadcasted_iota(jnp.int32, (blk, blk), 0) <= lax.broadcasted_iota(jnp.int32, (blk, blk), 1)
     live = lax.broadcasted_iota(jnp.int32, (PAD, blk), 0) < plen
-    pk_sum = pv_sum = None
     pk_parts, pv_parts = [], []
-    for i in range(slots):
+    add = lambda a, b: b if a is None else a + b
+
+    def scores(i, h):
+        lo, hi = i * blk, (i + 1) * blk
+        q = q_ref[lo:hi, :] * jnp.asarray(scale, BF)
+        do = do_ref[lo:hi, :]
+        return dg(km[h, 0:hi, :], q, 1, 1), dg(vm[h, 0:hi, :], do, 1, 1)
+
+    def start(i):
         lo, hi = i * blk, (i + 1) * blk
         q = q_ref[lo:hi, :] * jnp.asarray(scale, BF)
         do = do_ref[lo:hi, :]
         kp = stack(jnp.where(single, pk_ref[0:PAD, :], pk_ref[i * PAD:(i + 1) * PAD, :]))
         vp = stack(jnp.where(single, pv_ref[0:PAD, :], pv_ref[i * PAD:(i + 1) * PAD, :]))
-        sp = dg(kp, q, 1, 1)
-        dpp = dg(vp, do, 1, 1)
         prod = (do.astype(F) * o_ref[lo:hi, :].astype(F)).T
-        qs = split(q)
-        dos = split(do)
-        dqs, dsps = [], []
-        dk_new = dv_new = None
-        add = lambda a, b: b if a is None else a + b
-        pkp = pvp = None
-        offk = offv = diak = diav = None
-        for h in range(2):
-            lse = lse_ref[0, h:h + 1, lo:hi]
-            delta = jnp.sum(prod[h * hd:(h + 1) * hd], axis=0, keepdims=True)
-            p_pre = jnp.where(live, jnp.exp(sp[h * PAD:(h + 1) * PAD] - lse), 0.0)
-            ds_pre = (p_pre * (dpp[h * PAD:(h + 1) * PAD] - delta)).astype(BF)
-            p_dia = jnp.where(tri, jnp.exp(dg(km[h, lo:hi, :], q, 1, 1) - lse), 0.0)
-            ds_dia = (p_dia * (dg(vm[h, lo:hi, :], do, 1, 1) - delta)).astype(BF)
-            diav = add(diav, dg(p_dia.astype(BF), dos[h], 1, 0))
-            diak = add(diak, dg(ds_dia, qs[h], 1, 0))
-            pvp = add(pvp, dg(p_pre.astype(BF), dos[h], 1, 0))
-            pkp = add(pkp, dg(ds_pre, qs[h], 1, 0))
-            dqt = dg(kt[h * hd:(h + 1) * hd, lo:hi], ds_dia, 1, 0)
-            if i:
-                p_off = jnp.exp(dg(km[h, 0:lo, :], q, 1, 1) - jnp.where(single, lse, -NEG))
-                ds_off = (p_off * (dg(vm[h, 0:lo, :], do, 1, 1) - delta)).astype(BF)
-                offv = add(offv, dg(p_off.astype(BF), dos[h], 1, 0))
-                offk = add(offk, dg(ds_off, qs[h], 1, 0))
-                dqt = dqt + dg(kt[h * hd:(h + 1) * hd, 0:lo], ds_off, 1, 0)
-            dqs.append(dqt)
-            dsps.append(ds_pre)
-        dqt = jnp.concatenate(dqs, axis=0) + dg(kp.T, jnp.concatenate(dsps, axis=0), 1, 0)
+        return dict(q=split(q), do=split(do), kp=kp, sp=dg(kp, q, 1, 1), dpp=dg(vp, do, 1, 1), prod=prod,
+                    dqs=[], dsps=[], dk=None, dv=None, pk=None, pv=None)
+
+    def elem(i, h, st, s, dp):
+        lo, hi = i * blk, (i + 1) * blk
+        lse = lse_ref[0, h:h + 1, lo:hi]
+        delta = jnp.sum(st["prod"][h * hd:(h + 1) * hd], axis=0, keepdims=True)
+        p_pre = jnp.where(live, jnp.exp(st["sp"][h * PAD:(h + 1) * PAD] - lse), 0.0)
+        ds_pre = (p_pre * (st["dpp"][h * PAD:(h + 1) * PAD] - delta)).astype(BF)
+        p = jnp.where(tri, jnp.exp(s[lo:] - lse), 0.0)
+        ds = (p * (dp[lo:] - delta)).astype(BF)
+        p = p.astype(BF)
+        if i:
+            p_off = jnp.exp(s[:lo] - jnp.where(single, lse, -NEG))
+            ds_off = (p_off * (dp[:lo] - delta)).astype(BF)
+            p = jnp.concatenate([p_off.astype(BF), p], axis=0)
+            ds = jnp.concatenate([ds_off, ds], axis=0)
+        return p, ds, p_pre.astype(BF), ds_pre
+
+    def grads(i, h, st, p, ds, p_pre, ds_pre):
+        lo, hi = i * blk, (i + 1) * blk
+        st["dv"] = add(st["dv"], dg(p, st["do"][h], 1, 0))
+        st["dk"] = add(st["dk"], dg(ds, st["q"][h], 1, 0))
+        st["pv"] = add(st["pv"], dg(p_pre, st["do"][h], 1, 0))
+        st["pk"] = add(st["pk"], dg(ds_pre, st["q"][h], 1, 0))
+        st["dqs"].append(dg(kt[h * hd:(h + 1) * hd, 0:hi], ds, 1, 0))
+        st["dsps"].append(ds_pre)
+
+    def finish(i, st):
+        lo, hi = i * blk, (i + 1) * blk
+        dqt = jnp.concatenate(st["dqs"], axis=0) + dg(st["kp"].T, jnp.concatenate(st["dsps"], axis=0), 1, 0)
         dq_ref[lo:hi, :] = (dqt.T * scale).astype(BF)
-        dka[lo:hi, :] = diak
-        dva[lo:hi, :] = diav
+        dka[lo:hi, :] = st["dk"][lo:]
+        dva[lo:hi, :] = st["dv"][lo:]
         if i:
-            dka[0:lo, :] += offk
-            dva[0:lo, :] += offv
-        pk_parts.append(pkp)
-        pv_parts.append(pvp)
+            dka[0:lo, :] += st["dk"][:lo]
+            dva[0:lo, :] += st["dv"][:lo]
+        pk_parts.append(st["pk"])
+        pv_parts.append(st["pv"])
+
+    items = [(i, h) for i in range(slots) for h in range(2)]
+    sts = {}
+    def sc(n):
+        i, h = items[n]
+        if i not in sts: sts[i] = start(i)
+        return scores(i, h)
+    nxt = sc(0)
+    for n, (i, h) in enumerate(items):
+        cur = nxt
+        if n + 1 < len(items):
+            nxt = sc(n + 1)
+        grads(i, h, sts[i], *elem(i, h, sts[i], *cur))
+        if h:
+            finish(i, sts[i])
     dk_ref[...] = dka[...].astype(BF)
     dv_ref[...] = dva[...].astype(BF)
     for i in range(slots):
@@ -203,11 +159,23 @@
     return barrier, me, total
 
 
-def front_kernel(nt, nb, td, plen, chunk, cuts,
-                 ids_ref, emb_ref, ib_ref, ob_ref, g_ref, b_ref, tok_hbm, w_hbm, inner_hbm, outer_hbm,
-                 qkv_hbm, pkv_ref, hid_ref, low_ref,
-                 tok, w, inner, outer, normed, qkv, pre, emf, ibf, tbl, rs_out, rs_in, ag_out, ag_in, aa_out, aa_in,
-                 ld_sem, st_sem, rs_ss, rs_rs, ag_ss, ag_rs, aa_ss, aa_rs):
+def spread_heads(block, heads, hd):
+    wide = jnp.concatenate([block] * heads, axis=0)
+    row = lax.broadcasted_iota(jnp.int32, wide.shape, 0) // PAD
+    lane = lax.broadcasted_iota(jnp.int32, wide.shape, 1) // hd
+    return jnp.where(row == lane, wide, jnp.zeros((), wide.dtype))
+
+
+def prefix_rows(ref, single, i, lo, hi):
+    own = ref[pl.ds(pl.multiple_of(i * PAD, PAD), PAD), lo:hi]
+    return jnp.where(single, ref[0:PAD, lo:hi], own)
+
+
+def front_kernel(nt, nb, td, plen, chunk,
+                 ids_ref, len_ref, emb_ref, ib_ref, ob_ref, g_ref, b_ref, tok_hbm, w_hbm, inner_hbm, outer_hbm,
+                 qkv_hbm, att_hbm, pkv_ref, hid_ref, low_ref, lse_ref,
+                 tok, w, inner, outer, normed, qkv, ot_s, km, top_s, sum_s, pre, emf, ibf, tbl, rs_out, rs_in, ag_out, ag_in, aa_out, aa_in,
+                 ld_sem, st_sem, at_sem, rs_ss, rs_rs, ag_ss, ag_rs, aa_ss, aa_rs):
     rows, width = tok.shape
     slots = ids_ref.shape[0]
     rc = td * PAD // nb
@@ -262,8 +230,7 @@
         return c
 
     steps = w.shape[1] // chunk
-    c1, c2 = cuts
-    lax.fori_loop(0, c1, mm_step, 0)
+    lax.fori_loop(0, steps - 1, mm_step, 0)
     mine = pl.ds(pl.multiple_of(mb * rc, rc), rc)
     own = pre[mine, :] + ibf[mine, :]
     for c in rs_copy:
@@ -276,25 +243,14 @@
     ag_copy = [batch_copy(d, lambda to: ag_out, ag_in.at[d], ag_ss, ag_rs) for d in range(1, nb)]
     for c in ag_copy:
         c.start()
-    lax.fori_loop(c1, c2, mm_step, 0)
+    lax.fori_loop(steps - 1, steps, mm_step, 0)
 
     def put_low(frm, block):
         low_ref[pl.ds(pl.multiple_of(frm * rc, rc), rc), :] = block
 
-    put_low(mb, ag_out[0:rc, :])
-    for c in ag_copy:
-        c.wait_recv()
-    for d in range(1, nb):
-        put_low(lax.rem(mb + nb - d, nb), ag_in[d, 0:rc, :])
-    loads[3].wait()
-    ob = ob_ref[...].astype(F)
-    for t in range(td):
-        tbl[t] = (dg(low_ref[t * PAD:(t + 1) * PAD, :], outer[t], 1, 0) + ob[t:t + 1]).astype(BF)
-
-    def aa_copy(d):
-        to = lax.rem(me + d, total)
-        return pltpu.make_async_remote_copy(src_ref=aa_out.at[to], dst_ref=aa_in.at[me], send_sem=aa_ss.at[d],
-                                            recv_sem=aa_rs.at[me], device_id=peer_id(to, nb), device_id_type=MESH)
+    def aa_copy(d, to, at):
+        return pltpu.make_async_remote_copy(src_ref=aa_out.at[to], dst_ref=aa_in.at[at], send_sem=aa_ss.at[d],
+                                            recv_sem=aa_rs.at[at], device_id=peer_id(to, nb), device_id_type=MESH)
 
     def pick(e):
         idx = jnp.int32(0)
@@ -303,20 +259,77 @@
             idx = jnp.where(tid // td == mt, lax.rem(tid, td), idx)
         return tbl[idx]
 
-    def aa_step(d, c):
-        to = lax.rem(me + d, total)
-        aa_out[to] = pick(to)
-        aa_copy(d).start()
-        return c
-
-    lax.fori_loop(1, total, aa_step, 0)
-    aa_in[me] = pick(me)
-    lax.fori_loop(c2, steps, mm_step, 0)
+    def send_table():
+        put_low(mb, ag_out[0:rc, :])
+        for c in ag_copy:
+            c.wait_recv()
+        for d in range(1, nb):
+            put_low(lax.rem(mb + nb - d, nb), ag_in[d, 0:rc, :])
+        loads[3].wait()
+        ob = ob_ref[...].astype(F)
+        for t in range(td):
+            tbl[t] = (dg(low_ref[t * PAD:(t + 1) * PAD, :], outer[t], 1, 0) + ob[t:t + 1]).astype(BF)
+
+        def aa_step(d, c):
+            to = lax.rem(me + d, total)
+            aa_out[to] = pick(to)
+            aa_copy(d, to, me).start()
+            return c
+
+        lax.fori_loop(1, total, aa_step, 0)
+        aa_in[me] = pick(me)
+
+    blk = rows // slots
+    hd = 64
+    pair = 2 * hd
+    pairs = width // pair
+    scale = hd ** -0.5
+    single = len_ref[0, 0] > blk
+    first = lax.broadcasted_iota(jnp.int32, (1, pair), 1) < hd
+    zero = jnp.zeros((), BF)
+    tri = lax.broadcasted_iota(jnp.int32, (blk, blk), 0) <= lax.broadcasted_iota(jnp.int32, (blk, blk), 1)
+
+    def attend(h, c):
+        pl.when(h == 1)(send_table)
+        part = lambda third: qkv[:, pl.ds(pl.multiple_of(third * width + h * pair, pair), pair)]
+        q_all = part(0) * jnp.asarray(scale, BF)
+        k = part(1)
+        km[0] = jnp.where(first, k, zero)
+        km[1] = jnp.where(first, zero, k)
+        vt = part(2).T
+
+        def scores(i):
+            q = q_all[i * blk:(i + 1) * blk]
+            return [dg(km[j, 0:(i + 1) * blk, :], q, 1, 1) for j in range(2)]
+
+        nxt = scores(0)
+        for i in range(slots):
+            lo, hi = i * blk, (i + 1) * blk
+            cur = nxt
+            if i + 1 < slots:
+                nxt = scores(i + 1)
+            for j, s in enumerate(cur):
+                s_dia = jnp.where(tri, s[lo:], NEG)
+                top = jnp.max(s_dia, axis=0, keepdims=True)
+                if i:
+                    top = jnp.maximum(top, jnp.where(single, jnp.max(s[:lo], axis=0, keepdims=True), NEG))
+                p = jnp.exp(s_dia - top)
+                tot = jnp.sum(p, axis=0, keepdims=True)
+                p = p.astype(BF)
+                if i:
+                    p_off = jnp.exp(s[:lo] - jnp.where(single, top, -NEG))
+                    tot = tot + jnp.sum(p_off, axis=0, keepdims=True)
+                    p = jnp.concatenate([p_off.astype(BF), p], axis=0)
+                ot_s[pl.ds(pl.multiple_of(h * pair + j * hd, hd), hd), lo:hi] = dg(vt[j * hd:(j + 1) * hd, 0:hi], p, 1, 0)
+                top_s[h, j:j + 1, lo:hi] = top
+                sum_s[h, j:j + 1, lo:hi] = tot
+        return c
+
+    lax.fori_loop(0, pairs, attend, 0)
 
     def aa_wait(d, c):
         frm = lax.rem(me + d, total)
-        pltpu.make_async_remote_copy(src_ref=aa_out.at[frm], dst_ref=aa_in.at[frm], send_sem=aa_ss.at[d],
-                                     recv_sem=aa_rs.at[frm], device_id=peer_id(frm, nb), device_id_type=MESH).wait()
+        aa_copy(d, frm, frm).wait()
         return c
 
     lax.fori_loop(1, total, aa_wait, 0)
@@ -324,17 +337,51 @@
         owner = ids_ref[s, me] // td
         for b in range(nb):
             pkv_ref[s * PAD:(s + 1) * PAD, b * pc:(b + 1) * pc] = aa_in[owner * nb + b]
+    heads = 2 * pairs
+
+    def rows_of(i):
+        return pl.ds(pl.multiple_of(i * blk, blk), blk)
+
+    def att_store(i):
+        return pltpu.make_async_copy(normed.at[rows_of(i), :], att_hbm.at[rows_of(i), :], at_sem.at[i])
+
+    def merge(i, c):
+        cols = rows_of(i)
+        spread = lambda x: spread_heads(x, heads, hd)
+        q = qkv[cols, 0:width] * jnp.asarray(scale, BF)
+        sp = dg(spread(prefix_rows(pkv_ref, single, i, 0, width)), q, 1, 1)
+        live = lax.broadcasted_iota(jnp.int32, (PAD, blk), 0) < plen
+        ps, alphas, invs = [], [], []
+        for hh in range(heads):
+            s = jnp.where(live, sp[hh * PAD:(hh + 1) * PAD], NEG)
+            told = top_s[hh // 2, hh % 2:hh % 2 + 1, cols]
+            top = jnp.maximum(told, jnp.max(s, axis=0, keepdims=True))
+            p = jnp.exp(s - top)
+            alpha = jnp.exp(told - top)
+            tot = alpha * sum_s[hh // 2, hh % 2:hh % 2 + 1, cols] + jnp.sum(p, axis=0, keepdims=True)
+            lse_ref[hh // 2, hh % 2:hh % 2 + 1, cols] = top + jnp.log(tot)
+            inv = 1.0 / tot
+            ps.append(p.astype(BF))
+            alphas.append(alpha * inv)
+            invs.append(inv)
+        vt = spread(prefix_rows(pkv_ref, single, i, width, 2 * width)).T
+        pre = dg(vt, jnp.concatenate(ps, axis=0), 1, 0)
+        outs = [ot_s[hh * hd:(hh + 1) * hd, cols] * alphas[hh] + pre[hh * hd:(hh + 1) * hd] * invs[hh]
+                for hh in range(heads)]
+        normed[cols, :] = jnp.concatenate(outs, axis=0).T.astype(BF)
+        att_store(i).start()
+        return c
+
+    lax.fori_loop(0, slots, merge, 0)
     for c in rs_copy + ag_copy:
         c.wait_send()
-
-    def st_wait(j, c):
+    for j in range(steps):
         store(j).wait()
-        return c
-
-    lax.fori_loop(0, steps, st_wait, 0)
-
-
-def front(nt, nb, task_ids, prefix_embed, inner, inner_bias, outer, outer_bias, gain, bias, tokens, weight):
+    for i in range(slots):
+        att_store(i).wait()
+
+
+def front(nt, nb, task_ids, lengths, prefix_embed, inner, inner_bias, outer, outer_bias, gain, bias, tokens, weight):
     plen, td, depth = prefix_embed.shape
     rep = inner.shape[2]
     pc = outer.shape[2]
@@ -345,29 +392,30 @@
     rb = max(rc, PAD)
     chunk = 1024
     steps = weight.shape[1] // chunk
-    cuts = (steps // 3, 2 * steps // 3)
     sds = jax.ShapeDtypeStruct
     vm = pl.BlockSpec(memory_space=pltpu.VMEM)
     hb = pl.BlockSpec(memory_space=pl.ANY)
     dma = pltpu.SemaphoreType.DMA
     return pl.pallas_call(
-        functools.partial(front_kernel, nt, nb, td, plen, chunk, cuts),
-        in_specs=[pl.BlockSpec(memory_space=pltpu.SMEM), vm, vm, vm, vm, vm, hb, hb, hb, hb],
-        out_specs=[hb, vm, vm, vm],
-        out_shape=[sds((rows, weight.shape[1]), BF), sds((slots * PAD, nb * pc), BF), sds((rc, rep), F),
-                   sds((td * PAD, rep), BF)],
+        functools.partial(front_kernel, nt, nb, td, plen, chunk),
+        in_specs=[pl.BlockSpec(memory_space=pltpu.SMEM)] * 2 + [vm] * 5 + [hb] * 4,
+        out_specs=[hb, hb, vm, vm, vm, vm],
+        out_shape=[sds((rows, weight.shape[1]), BF), sds((rows, width), BF), sds((slots * PAD, nb * pc), BF), sds((rc, rep), F),
+                   sds((td * PAD, rep), BF), sds((width // 128, 2, rows), F)],
         scratch_shapes=[
             pltpu.VMEM((rows, width), BF), pltpu.VMEM(weight.shape, BF), pltpu.VMEM(inner.shape, BF),
             pltpu.VMEM(outer.shape, BF), pltpu.VMEM((rows, width), BF), pltpu.VMEM((rows, weight.shape[1]), BF),
+            pltpu.VMEM((width, rows), F), pltpu.VMEM((2, rows, 128), BF),
+            pltpu.VMEM((width // 128, 2, rows), F), pltpu.VMEM((width // 128, 2, rows), F),
             pltpu.VMEM((td * PAD, rep), F), pltpu.VMEM((plen * td, depth), F), pltpu.VMEM((td * PAD, rep), F), pltpu.VMEM((td, PAD, pc), BF),
             pltpu.VMEM((nb, rb, rep), BF), pltpu.VMEM((nb, rb, rep), BF),
             pltpu.VMEM((rb, rep), BF), pltpu.VMEM((nb, rb, rep), BF),
             pltpu.VMEM((total, PAD, pc), BF), pltpu.VMEM((total, PAD, pc), BF),
-            dma((4,)), dma((steps,)), dma((nb,)), dma((nb,)), dma((nb,)), dma((nb,)), dma((total,)), dma((total,)),
+            dma((4,)), dma((steps,)), dma((slots,)), dma((nb,)), dma((nb,)), dma((nb,)), dma((nb,)), dma((total,)), dma((total,)),
         ],
         compiler_params=pltpu.CompilerParams(vmem_limit_bytes=62 * 2**20, collective_id=0, has_side_effects=True),
-        name="front",
-    )(task_ids, prefix_embed, inner_bias, outer_bias, gain, bias,
+        name="front_attend",
+    )(task_ids, lengths, prefix_embed, inner_bias, outer_bias, gain, bias,
       tokens, weight, inner, outer)
 
 
@@ -697,11 +745,10 @@
     batch_count = lax.axis_size("batch")
     ids = task_ids.T
     embed = prefix_embed.transpose(1, 0, 2)
-    projected, prefix_kv, hidden_chunk, hidden_low = front(
-        task_count, batch_count, ids, embed, reparam_inner, reparam_inner_bias, reparam_outer,
+    projected, attended, prefix_kv, hidden_chunk, hidden_low, log_totals = front(
+        task_count, batch_count, ids, lengths, embed, reparam_inner, reparam_inner_bias, reparam_outer,
         reparam_outer_bias, first_gain, first_bias, tokens, input_weight,
     )
-    attended, log_totals = attn_fwd(lengths, projected, prefix_kv, prefix_len)
     output, grad_mid, grad_attended = middle(
         second_gain, second_bias, tokens, attended, output_cotangent, output_weight, expand_weight, contract_weight
     )

time: 188 us -> 168 us (0.89)
  Pallas kernels: 186 us -> 167 us
    pallas_call x2 -> x1, Pallas kernels: 61.2 us -> 42.3 us  [front(): pl.pallas_call(functools.partial(front_kernel, nt, nb, td, plen, chunk),...]
    pallas_call x1, Pallas kernels: 37.8 us -> 33.9 us  [attn_bwd(): pl.pallas_call(functools.partial(attn_bwd_kernel, slots, plen), grid=(pai...]
    pallas_call x1, Pallas kernels: 27.8 us -> 30.9 us  [back(): pl.pallas_call(functools.partial(back_kernel, nt, nb, td, blk), in_specs=...]
where the time goes in v1:
time: 168 us; the launch traced here: 167 us
  Pallas kernels  167 us (99%)
    pallas_call x1, Pallas kernels, middle(): pl.pallas_call(functools.partial(middle_kernel, blk, fch), in_specs=[vm,...  49.9 us
    pallas_call x1, Pallas kernels, front(): pl.pallas_call(functools.partial(front_kernel, nt, nb, td, plen, chunk),...  42.3 us
    pallas_call x1, Pallas kernels, attn_bwd(): pl.pallas_call(functools.partial(attn_bwd_kernel, slots, plen), grid=(pai...  33.9 us
    pallas_call x1, Pallas kernels, back(): pl.pallas_call(functools.partial(back_kernel, nt, nb, td, blk), in_specs=...  30.9 us
    pallas_call x1, Pallas kernels, tail(): pl.pallas_call(functools.partial(tail_kernel, plen), grid=(td // per,), i...  9.71 us

profile of v1, /device:TPU:0, one launch (start us, length us, event | category | flops | bytes accessed | tf_op | source)
XLA Modules:
  0.0 167.4 jit_solution(14245185545912954547)
XLA Ops:
  0.6 42.3 %front_attend.1 = (bf16[1024,3072]{1,0:T(8,128)(2,1)}, bf16[1024,1024]{1,0:T(8,128)(2,1)}, bf16[64,2048]{1,0:T(8,128)(2,1)}, f32[32,512]{1,0:T(8,128)}, bf16[256,512]{1,0:T(8,128)(2,1)}, /*index=5*/f32[8,2,1024]{2,1,0:T(2,128)}) custom-call(s32[4,32]{1,0:T(4,128)} %bitcast.11, s32[1,4]{1,0:T(1,128)} %len_ref.3, bf16[10,16,128]{2,1,0:T(8,128)(2,1)} %bitcast.9, ...), custom_call_target="tpu_custom_call" | custom-call | tf_op jit(solution)/shard_map/front_attend/pallas_call | solution.py:399
  43.0 49.9 %middle.1 = (bf16[1024,1024]{1,0:T(8,128)(2,1)}, f32[1024,1024]{1,0:T(8,128)}, bf16[1024,1024]{1,0:T(8,128)(2,1)}) custom-call(bf16[1024]{0:T(1024)(128)(2,1)} %g_ref.4, bf16[1024]{0:T(1024)(128)(2,1)} %b_ref.3, bf16[1024,1024]{1,0:T(8,128)(2,1)} %tok_hbm.5, bf16[1024,1024]{1,0:T(8,128)(2,1)} %get-tuple-element.30.att_hbm.o_ref, bf16[1024,1024]{1,0:T(8,128)(2,1)} %ct_hbm.1, ...), custom_call_target="tpu_custom_call" | custom-call | tf_op jit(solution)/shard_map/middle/pallas_call | solution.py:508
  92.9 33.9 %attend_back.1 = (bf16[1024,1024]{1,0:T(8,128)(2,1)}, bf16[1024,1024]{1,0:T(8,128)(2,1)}, bf16[1024,1024]{1,0:T(8,128)(2,1)}, f32[64,1024]{1,0:T(8,128)}, f32[64,1024]{1,0:T(8,128)}) custom-call(s32[1,4]{1,0:T(1,128)} %len_ref.3, bf16[1024,3072]{1,0:T(8,128)(2,1)} %get-tuple-element.33.q_ref.k_ref.v_ref, ...), custom_call_target="tpu_custom_call" | custom-call | tf_op jit(solution)/shard_map/attend_back/pallas_call | solution.py:124
  126.9 30.9 %back.1 = (bf16[1024,1024]{1,0:T(8,128)(2,1)}, bf16[256,512]{1,0:T(8,128)(2,1)}, bf16[256,256]{1,0:T(8,128)(2,1)}) custom-call(s32[4,32]{1,0:T(4,128)} %bitcast.12, f32[32,512]{1,0:T(8,128)} %get-tuple-element.32.hid_ref, bf16[1024]{0:T(1024)(128)(2,1)} %g_ref.5, f32[4,16,1024]{2,1,0:T(8,128)} %bitcast.7, f32[4,16,1024]{2,1,0:T(8,128)} %bitcast.8, ...), custom_call_target="tpu_custom_call" | custom-call | tf_op jit(solution)/shard_map/back/pallas_call | solution.py:656
  157.7 9.7 %tail.1 = (bf16[1024,1024]{1,0:T(8,128)(2,1)}, f32[160,128]{1,0:T(8,128)}, f32[16,128,512]{2,1,0:T(8,128)}, f32[16,512]{1,0:T(8,128)}, f32[16,512,256]{2,1,0:T(8,128)}, /*index=5*/f32[16,256]{1,0:T(8,128)}) custom-call(bf16[1024,1024]{1,0:T(8,128)(2,1)} %get-tuple-element.43.ig_in, bf16[10,16,128]{2,1,0:T(8,128)(2,1)} %bitcast.10, ...), custom_call_target="tpu_custom_call" | custom-call | tf_op jit(solution)/shard_map/tail/pallas_call | solution.py:711

commit v2 on v1

--- a/solution.py
+++ b/solution.py
@@ -16,122 +16,6 @@
 
 def dg(a, b, ca, cb):
     return lax.dot_general(a, b, (((ca,), (cb,)), ((), ())), preferred_element_type=F)
-
-
-def attn_bwd_kernel(slots, plen, len_ref, q_ref, k_ref, v_ref, pk_ref, pv_ref, o_ref, do_ref, lse_ref,
-                    dq_ref, dk_ref, dv_ref, dpk_ref, dpv_ref, km, vm, dka, dva):
-    rows, pair = q_ref.shape
-    blk = rows // slots
-    hd = pair // 2
-    scale = hd ** -0.5
-    single = len_ref[0, 0] > blk
-    first = lax.broadcasted_iota(jnp.int32, (1, pair), 1) < hd
-    zero = jnp.zeros((), BF)
-    split = lambda a: (jnp.where(first, a, zero), jnp.where(first, zero, a))
-    stack = lambda a: jnp.concatenate(split(a), axis=0)
-    k = k_ref[...]
-    km[0], km[1] = split(k)
-    vm[0], vm[1] = split(v_ref[...])
-    kt = k.T
-    tri = lax.broadcasted_iota(jnp.int32, (blk, blk), 0) <= lax.broadcasted_iota(jnp.int32, (blk, blk), 1)
-    live = lax.broadcasted_iota(jnp.int32, (PAD, blk), 0) < plen
-    pk_parts, pv_parts = [], []
-    add = lambda a, b: b if a is None else a + b
-
-    def scores(i, h):
-        lo, hi = i * blk, (i + 1) * blk
-        q = q_ref[lo:hi, :] * jnp.asarray(scale, BF)
-        do = do_ref[lo:hi, :]
-        return dg(km[h, 0:hi, :], q, 1, 1), dg(vm[h, 0:hi, :], do, 1, 1)
-
-    def start(i):
-        lo, hi = i * blk, (i + 1) * blk
-        q = q_ref[lo:hi, :] * jnp.asarray(scale, BF)
-        do = do_ref[lo:hi, :]
-        kp = stack(jnp.where(single, pk_ref[0:PAD, :], pk_ref[i * PAD:(i + 1) * PAD, :]))
-        vp = stack(jnp.where(single, pv_ref[0:PAD, :], pv_ref[i * PAD:(i + 1) * PAD, :]))
-        prod = (do.astype(F) * o_ref[lo:hi, :].astype(F)).T
-        return dict(q=split(q), do=split(do), kp=kp, sp=dg(kp, q, 1, 1), dpp=dg(vp, do, 1, 1), prod=prod,
-                    dqs=[], dsps=[], dk=None, dv=None, pk=None, pv=None)
-
-    def elem(i, h, st, s, dp):
-        lo, hi = i * blk, (i + 1) * blk
-        lse = lse_ref[0, h:h + 1, lo:hi]
-        delta = jnp.sum(st["prod"][h * hd:(h + 1) * hd], axis=0, keepdims=True)
-        p_pre = jnp.where(live, jnp.exp(st["sp"][h * PAD:(h + 1) * PAD] - lse), 0.0)
-        ds_pre = (p_pre * (st["dpp"][h * PAD:(h + 1) * PAD] - delta)).astype(BF)
-        p = jnp.where(tri, jnp.exp(s[lo:] - lse), 0.0)
-        ds = (p * (dp[lo:] - delta)).astype(BF)
-        p = p.astype(BF)
-        if i:
-            p_off = jnp.exp(s[:lo] - jnp.where(single, lse, -NEG))
-            ds_off = (p_off * (dp[:lo] - delta)).astype(BF)
-            p = jnp.concatenate([p_off.astype(BF), p], axis=0)
-            ds = jnp.concatenate([ds_off, ds], axis=0)
-        return p, ds, p_pre.astype(BF), ds_pre
-
-    def grads(i, h, st, p, ds, p_pre, ds_pre):
-        lo, hi = i * blk, (i + 1) * blk
-        st["dv"] = add(st["dv"], dg(p, st["do"][h], 1, 0))
-        st["dk"] = add(st["dk"], dg(ds, st["q"][h], 1, 0))
-        st["pv"] = add(st["pv"], dg(p_pre, st["do"][h], 1, 0))
-        st["pk"] = add(st["pk"], dg(ds_pre, st["q"][h], 1, 0))
-        st["dqs"].append(dg(kt[h * hd:(h + 1) * hd, 0:hi], ds, 1, 0))
-        st["dsps"].append(ds_pre)
-
-    def finish(i, st):
-        lo, hi = i * blk, (i + 1) * blk
-        dqt = jnp.concatenate(st["dqs"], axis=0) + dg(st["kp"].T, jnp.concatenate(st["dsps"], axis=0), 1, 0)
-        dq_ref[lo:hi, :] = (dqt.T * scale).astype(BF)
-        dka[lo:hi, :] = st["dk"][lo:]
-        dva[lo:hi, :] = st["dv"][lo:]
-        if i:
-            dka[0:lo, :] += st["dk"][:lo]
-            dva[0:lo, :] += st["dv"][:lo]
-        pk_parts.append(st["pk"])
-        pv_parts.append(st["pv"])
-
-    items = [(i, h) for i in range(slots) for h in range(2)]
-    sts = {}
-    def sc(n):
-        i, h = items[n]
-        if i not in sts: sts[i] = start(i)
-        return scores(i, h)
-    nxt = sc(0)
-    for n, (i, h) in enumerate(items):
-        cur = nxt
-        if n + 1 < len(items):
-            nxt = sc(n + 1)
-        grads(i, h, sts[i], *elem(i, h, sts[i], *cur))
-        if h:
-            finish(i, sts[i])
-    dk_ref[...] = dka[...].astype(BF)
-    dv_ref[...] = dva[...].astype(BF)
-    for i in range(slots):
-        for ref, parts in ((dpk_ref, pk_parts), (dpv_ref, pv_parts)):
-            whole = sum(parts) if i == 0 else jnp.zeros_like(parts[0])
-            ref[i * PAD:(i + 1) * PAD, :] = jnp.where(single, whole, parts[i])
-
-
-def attn_bwd(lengths, qkv, pkv, attended, grad_att, lse, plen):
-    rows = qkv.shape[0]
-    width = qkv.shape[1] // 3
-    slots = lengths.shape[1]
-    pairs = width // 128
-    col = lambda off: pl.BlockSpec((rows, 128), lambda h: (0, h + off))
-    pcol = lambda off: pl.BlockSpec((slots * PAD, 128), lambda h: (0, h + off))
-    sds = jax.ShapeDtypeStruct
-    return pl.pallas_call(
-        functools.partial(attn_bwd_kernel, slots, plen),
-        grid=(pairs,),
-        in_specs=[pl.BlockSpec(memory_space=pltpu.SMEM), col(0), col(pairs), col(2 * pairs), pcol(0), pcol(pairs),
-                  col(0), col(0), pl.BlockSpec((1, 2, rows), lambda h: (h, 0, 0))],
-        out_specs=[col(0), col(0), col(0), pcol(0), pcol(0)],
-        out_shape=[sds((rows, width), BF)] * 3 + [sds((slots * PAD, width), F)] * 2,
-        scratch_shapes=[pltpu.VMEM((2, rows, 128), BF)] * 2 + [pltpu.VMEM((rows, 128), F)] * 2,
-        compiler_params=pltpu.CompilerParams(vmem_limit_bytes=62 * 2**20),
-        name="attend_back",
-    )(lengths, qkv, qkv, qkv, pkv, pkv, attended, grad_att, lse)
 
 
 def peer_id(flat, nb):
@@ -518,27 +402,90 @@
     )(gain, bias, tokens, attended, ct, wo, we, wc)
 
 
-def back_kernel(nt, nb, td, blk,
-                ids_ref, hid_ref, g_ref, dpk_ref, dpv_ref, outer_hbm, w_hbm, dq_hbm, dk_hbm, dv_hbm, tok_hbm, gm_hbm,
+def back_kernel(nt, nb, td, plen, blk,
+                ids_ref, len_ref, hid_ref, g_ref, lse_ref, pkv_ref, outer_hbm, w_hbm, qkv_hbm, att_hbm, do_hbm, tok_hbm,
+                gm_hbm,
                 ig_hbm, gpre_ref, gtl_ref,
-                outer, w, dq, dk, dv, tok, gm, ig, sel, rs_out, rs_in, ag_out, ag_in, aa_out, aa_in, part,
-                ld_sem, st_sem, rs_ss, rs_rs, ag_ss, ag_rs, aa_ss, aa_rs):
+                outer, w, qkv, att, do_s, tok, gm, dqkv, dqp, km, vm, dka, dva, del_s, dpk_s, dpv_s, gbuf,
+                sel, rs_out, rs_in, ag_out, ag_in, aa_out, aa_in, part,
+                ld_sem, bl_sem, st_sem, rs_ss, rs_rs, ag_ss, ag_rs, aa_ss, aa_rs):
     rows, width = tok.shape
     slots = ids_ref.shape[0]
     rc = td * PAD // nb
     pc = outer.shape[2]
+    hd = 64
+    pair = 2 * hd
+    pairs = width // pair
+    heads = 2 * pairs
+    scale = hd ** -0.5
+    inv = 1.0 / width
+    single = len_ref[0, 0] > blk
     mt = lax.axis_index("task")
     mb = lax.axis_index("batch")
-    names = ((w_hbm, w), (dq_hbm, dq), (dk_hbm, dk), (dv_hbm, dv), (tok_hbm, tok), (gm_hbm, gm), (outer_hbm, outer))
+
+    def rows_of(i):
+        return pl.ds(pl.multiple_of(i * blk, blk), blk)
+
+    def block_loads(i):
+        r = rows_of(i)
+        return [pltpu.make_async_copy(s, d, bl_sem.at[k, i]) for k, (s, d) in enumerate((
+            (qkv_hbm.at[r, 0:width], qkv.at[r, 0:width]), (do_hbm.at[r, :], do_s.at[r, :]), (att_hbm.at[r, :], att.at[r, :])))]
+
+    rest = slice(width, 3 * width)
+    names = ((qkv_hbm.at[:, rest], qkv.at[:, rest]), (outer_hbm, outer), (w_hbm, w), (tok_hbm, tok), (gm_hbm, gm))
     loads = [pltpu.make_async_copy(s, d, ld_sem.at[i]) for i, (s, d) in enumerate(names)]
+    for i in range(slots):
+        for c in block_loads(i):
+            c.start()
     for c in loads:
         c.start()
     barrier, me, total = greet_all(nt, nb)
+    live = lax.broadcasted_iota(jnp.int32, (PAD, blk), 0) < plen
+    lane_head = lax.broadcasted_iota(jnp.int32, (heads, width), 1) // hd
+    picker = jnp.where(lane_head == lax.broadcasted_iota(jnp.int32, (heads, width), 0), 1.0, 0.0).astype(BF)
+    own_block = (lax.broadcasted_iota(jnp.int32, (heads * PAD, width), 0) // PAD
+                 == lax.broadcasted_iota(jnp.int32, (heads * PAD, width), 1) // hd)
+
+    def prefix_step(i, c):
+        cols = rows_of(i)
+        for cp in block_loads(i):
+            cp.wait()
+        q = qkv[cols, 0:width] * jnp.asarray(scale, BF)
+        do = do_s[cols, :]
+        prod = do.astype(F) * att[cols, :].astype(F)
+        high = prod.astype(BF)
+        delta = dg(picker, high, 1, 1) + dg(picker, (prod - high.astype(F)).astype(BF), 1, 1)
+        kp = spread_heads(prefix_rows(pkv_ref, single, i, 0, width), heads, hd)
+        vp = spread_heads(prefix_rows(pkv_ref, single, i, width, 2 * width), heads, hd)
+        sp = dg(kp, q, 1, 1)
+        dpp = dg(vp, do, 1, 1)
+        ps, dss = [], []
+        for hh in range(heads):
+            one = slice(hh * PAD, (hh + 1) * PAD)
+            del_s[hh // 2, hh % 2:hh % 2 + 1, cols] = delta[hh:hh + 1]
+            pr = jnp.where(live, jnp.exp(sp[one] - lse_ref[hh // 2, hh % 2:hh % 2 + 1, cols]), 0.0)
+            ps.append(pr.astype(BF))
+            dss.append((pr * (dpp[one] - delta[hh:hh + 1])).astype(BF))
+        ds = jnp.concatenate(dss, axis=0)
+        fold = lambda x: jnp.sum(jnp.where(own_block, x, 0.0).reshape(heads, PAD, width), axis=0)
+        dpk_s[i] = fold(dg(ds, q, 1, 0))
+        dpv_s[i] = fold(dg(jnp.concatenate(ps, axis=0), do, 1, 0))
+        dqp[:, cols] = dg(kp.T, ds, 1, 0)
+        return c
+
+    lax.fori_loop(0, slots, prefix_step, 0)
+    for ref in (dpk_s, dpv_s):
+        whole = ref[0]
+        for i in range(1, slots):
+            whole = whole + ref[i]
+        ref[0] = jnp.where(single, whole, ref[0])
+        for i in range(1, slots):
+            ref[i] = jnp.where(single, 0.0, ref[i])
     for o in range(nt):
         at = jnp.int32(0)
         for s in range(slots):
             at = jnp.where(ids_ref[s, me] // td == o, s, at)
-        for half, ref in enumerate((dpk_ref, dpv_ref)):
+        for half, ref in enumerate((dpk_s, dpv_s)):
             block = ref[at].astype(BF)
             for b in range(nb // 2):
                 aa_out[o * nb + half * (nb // 2) + b] = block[:, b * pc:(b + 1) * pc]
@@ -565,19 +512,112 @@
     want = task_of * PAD + lax.rem(lane, PAD)
     row = lax.broadcasted_iota(jnp.int32, (td * PAD, total * PAD), 0)
     sel[...] = jnp.where(row == want, 1.0, 0.0).astype(BF)
+
+    def batch_copy(d, src, dst, ss, rs):
+        to = lax.rem(mb + d, nb)
+        return pltpu.make_async_remote_copy(src_ref=src(to), dst_ref=dst, send_sem=ss.at[d], recv_sem=rs.at[d],
+                                            device_id={"task": mt, "batch": to}, device_id_type=MESH)
+
+    rs_copy = [batch_copy(d, lambda to: rs_out.at[to], rs_in.at[d], rs_ss, rs_rs) for d in range(1, nb)]
+    ag_copy = [batch_copy(d, lambda to: ag_out, ag_in.at[d], ag_ss, ag_rs) for d in range(1, nb)]
+
+    def sum_table():
+        def aa_wait(d, c):
+            frm = lax.rem(me + d, total)
+            aa_copy(d, frm, frm).wait()
+            return c
+
+        lax.fori_loop(1, total, aa_wait, 0)
+        gtl_ref[...] = dg(sel[...], aa_in[...].reshape(total * PAD, pc), 1, 0).astype(BF)
+        loads[1].wait()
+        for t in range(td):
+            part[t * PAD:(t + 1) * PAD, :] = dg(gtl_ref[t * PAD:(t + 1) * PAD, :], outer[t], 1, 1)
+        for c in range(nb):
+            rs_out[c, 0:rc, :] = part[c * rc:(c + 1) * rc, :].astype(BF)
+        for c in rs_copy:
+            c.start()
+
+    def sum_hidden():
+        own = part[pl.ds(pl.multiple_of(mb * rc, rc), rc), :]
+        for c in rs_copy:
+            c.wait_recv()
+        for d in range(1, nb):
+            own = own + rs_in[d, 0:rc, :].astype(F)
+        hid = hid_ref[...]
+        ag_out[0:rc, :] = (own * (1.0 - hid * hid)).astype(BF)
+        for c in ag_copy:
+            c.start()
+
+    loads[0].wait()
+    first = lax.broadcasted_iota(jnp.int32, (1, pair), 1) < hd
+    zero = jnp.zeros((), BF)
+    split = lambda a: (jnp.where(first, a, zero), jnp.where(first, zero, a))
+    tri = lax.broadcasted_iota(jnp.int32, (blk, blk), 0) <= lax.broadcasted_iota(jnp.int32, (blk, blk), 1)
+    add = lambda a, b: b if a is None else a + b
+
+    def attend(h, c):
+        pl.when(h == 2)(sum_table)
+        pl.when(h == 5)(sum_hidden)
+        cols_of = lambda third: pl.ds(pl.multiple_of(third * width + h * pair, pair), pair)
+        q_all = qkv[:, cols_of(0)] * jnp.asarray(scale, BF)
+        do_all = do_s[:, cols_of(0)]
+        k = qkv[:, cols_of(1)]
+        km[0], km[1] = split(k)
+        vm[0], vm[1] = split(qkv[:, cols_of(2)])
+        kt = k.T
+        qs, dos = split(q_all), split(do_all)
+
+        def scores(i, j):
+            lo, hi = i * blk, (i + 1) * blk
+            return dg(km[j, 0:hi, :], q_all[lo:hi], 1, 1), dg(vm[j, 0:hi, :], do_all[lo:hi], 1, 1)
+
+        items = [(i, j) for i in range(slots) for j in range(2)]
+        nxt = scores(*items[0])
+        for n, (i, j) in enumerate(items):
+            lo, hi = i * blk, (i + 1) * blk
+            s, dp = nxt
+            if n + 1 < len(items):
+                nxt = scores(*items[n + 1])
+            lse = lse_ref[h, j:j + 1, lo:hi]
+            delta = del_s[h, j:j + 1, lo:hi]
+            p = jnp.where(tri, jnp.exp(s[lo:] - lse), 0.0)
+            ds = (p * (dp[lo:] - delta)).astype(BF)
+            p = p.astype(BF)
+            if i:
+                off = jnp.exp(s[:lo] - jnp.where(single, lse, -NEG))
+                ds = jnp.concatenate([(off * (dp[:lo] - delta)).astype(BF), ds], axis=0)
+                p = jnp.concatenate([off.astype(BF), p], axis=0)
+            if j == 0:
+                dk = dv = None
+                dqs = []
+            dv = add(dv, dg(p, dos[j][lo:hi], 1, 0))
+            dk = add(dk, dg(ds, qs[j][lo:hi], 1, 0))
+            dqs.append(dg(kt[j * hd:(j + 1) * hd, 0:hi], ds, 1, 0))
+            if j:
+                dqt = jnp.concatenate(dqs, axis=0) + dqp[pl.ds(pl.multiple_of(h * pair, pair), pair), lo:hi]
+                dqkv[lo:hi, cols_of(0)] = (dqt.T * scale).astype(BF)
+                dka[lo:hi, :] = dk[lo:]
+                dva[lo:hi, :] = dv[lo:]
+                if i:
+                    dka[0:lo, :] += dk[:lo]
+                    dva[0:lo, :] += dv[:lo]
+        dqkv[:, cols_of(1)] = dka[...].astype(BF)
+        dqkv[:, cols_of(2)] = dva[...].astype(BF)
+        return c
+
+    lax.fori_loop(0, pairs, attend, 0)
     gain = g_ref[...].astype(F).reshape(1, -1)
-    for c in loads[:6]:
+    for c in loads[2:]:
         c.wait()
-    inv = 1.0 / width
 
     def store(i):
-        r = pl.ds(pl.multiple_of(i * blk, blk), blk)
-        return pltpu.make_async_copy(ig.at[r, :], ig_hbm.at[r, :], st_sem.at[i])
-
-    def mm_step(i, c):
-        r = pl.ds(pl.multiple_of(i * blk, blk), blk)
-        gn = (dg(dq[r, :], w[:, 0:width], 1, 1) + dg(dk[r, :], w[:, width:2 * width], 1, 1)
-              + dg(dv[r, :], w[:, 2 * width:], 1, 1))
+        return pltpu.make_async_copy(tok.at[rows_of(i), :], ig_hbm.at[rows_of(i), :], st_sem.at[i])
+
+    def product(i):
+        return dg(dqkv[rows_of(i), :], w[...], 1, 1)
+
+    def norm_back(i, gn):
+        r = rows_of(i)
         ug = gn * gain
         x = tok[r, :].astype(F)
         cen = x - jnp.sum(x, axis=1, keepdims=True) * inv
@@ -585,47 +625,18 @@
         xhat = cen * rstd
         m1 = jnp.sum(ug, axis=1, keepdims=True) * inv
         m2 = jnp.sum(ug * xhat, axis=1, keepdims=True) * inv
-        ig[r, :] = (gm[r, :] + rstd * (ug - m1 - xhat * m2)).astype(BF)
+        tok[r, :] = (gm[r, :] + rstd * (ug - m1 - xhat * m2)).astype(BF)
         store(i).start()
-        return c
-
-    steps = rows // blk
-    c1, c2 = steps // 4, 3 * steps // 4
-    lax.fori_loop(0, c1, mm_step, 0)
-
-    def aa_wait(d, c):
-        frm = lax.rem(me + d, total)
-        aa_copy(d, frm, frm).wait()
-        return c
-
-    lax.fori_loop(1, total, aa_wait, 0)
-    gtl_ref[...] = dg(sel[...], aa_in[...].reshape(total * PAD, pc), 1, 0).astype(BF)
-    loads[6].wait()
-    for t in range(td):
-        part[t * PAD:(t + 1) * PAD, :] = dg(gtl_ref[t * PAD:(t + 1) * PAD, :], outer[t], 1, 1)
-    for c in range(nb):
-        rs_out[c, 0:rc, :] = part[c * rc:(c + 1) * rc, :].astype(BF)
-
-    def batch_copy(d, src, dst, ss, rs):
-        to = lax.rem(mb + d, nb)
-        return pltpu.make_async_remote_copy(src_ref=src(to), dst_ref=dst, send_sem=ss.at[d], recv_sem=rs.at[d],
-                                            device_id={"task": mt, "batch": to}, device_id_type=MESH)
-
-    rs_copy = [batch_copy(d, lambda to: rs_out.at[to], rs_in.at[d], rs_ss, rs_rs) for d in range(1, nb)]
-    for c in rs_copy:
-        c.start()
-    lax.fori_loop(c1, c2, mm_step, 0)
-    own = part[pl.ds(pl.multiple_of(mb * rc, rc), rc), :]
-    for c in rs_copy:
-        c.wait_recv()
-    for d in range(1, nb):
-        own = own + rs_in[d, 0:rc, :].astype(F)
-    hid = hid_ref[...]
-    ag_out[0:rc, :] = (own * (1.0 - hid * hid)).astype(BF)
-    ag_copy = [batch_copy(d, lambda to: ag_out, ag_in.at[d], ag_ss, ag_rs) for d in range(1, nb)]
-    for c in ag_copy:
-        c.start()
-    lax.fori_loop(c2, steps, mm_step, 0)
+
+    gbuf[0] = product(0)
+
+    def mm_step(i, c):
+        gbuf[lax.rem(i, 2)] = product(i)
+        norm_back(i - 1, gbuf[lax.rem(i + 1, 2)])
+        return c
+
+    lax.fori_loop(1, slots, mm_step, 0)
+    norm_back(slots - 1, gbuf[(slots - 1) % 2])
 
     def put(frm, block):
         gpre_ref[pl.ds(pl.multiple_of(frm * rc, rc), rc), :] = block
@@ -637,41 +648,45 @@
         put(lax.rem(mb + nb - d, nb), ag_in[d, 0:rc, :])
     for c in rs_copy + ag_copy:
         c.wait_send()
-    for i in range(steps):
+    for i in range(slots):
         store(i).wait()
 
 
-def back(nt, nb, task_ids, hid, gain, dpk, dpv, outer, weight, dq, dk, dv, tokens, grad_mid):
+def back(nt, nb, task_ids, lengths, hid, gain, lse, pkv, outer, weight, qkv, attended, grad_att, tokens, grad_mid, plen):
     td, rep, pc = outer.shape
     rows, width = tokens.shape
     slots = task_ids.shape[0]
     total = nt * nb
     rc = td * PAD // nb
     rb = max(rc, PAD)
-    blk = 256
+    blk = rows // slots
     sds = jax.ShapeDtypeStruct
     vm = pl.BlockSpec(memory_space=pltpu.VMEM)
     hb = pl.BlockSpec(memory_space=pl.ANY)
     dma = pltpu.SemaphoreType.DMA
+    full = lambda t: pltpu.VMEM((rows, width), t)
     return pl.pallas_call(
-        functools.partial(back_kernel, nt, nb, td, blk),
-        in_specs=[pl.BlockSpec(memory_space=pltpu.SMEM), vm, vm, vm, vm] + [hb] * 7,
+        functools.partial(back_kernel, nt, nb, td, plen, blk),
+        in_specs=[pl.BlockSpec(memory_space=pltpu.SMEM)] * 2 + [vm] * 4 + [hb] * 7,
         out_specs=[hb, vm, vm],
         out_shape=[sds((rows, width), BF), sds((td * PAD, rep), BF), sds((td * PAD, pc), BF)],
         scratch_shapes=[
-            pltpu.VMEM(outer.shape, BF), pltpu.VMEM(weight.shape, BF)] + [pltpu.VMEM((rows, width), BF)] * 4 + [
-            pltpu.VMEM((rows, width), F), pltpu.VMEM((rows, width), BF),
+            pltpu.VMEM(outer.shape, BF), pltpu.VMEM(weight.shape, BF), pltpu.VMEM(qkv.shape, BF), full(BF), full(BF),
+            full(BF), full(F), pltpu.VMEM(qkv.shape, BF), pltpu.VMEM((width, rows), F),
+            pltpu.VMEM((2, rows, 128), BF), pltpu.VMEM((2, rows, 128), BF), pltpu.VMEM((rows, 128), F),
+            pltpu.VMEM((rows, 128), F), pltpu.VMEM(lse.shape, F), pltpu.VMEM((slots, PAD, width), F),
+            pltpu.VMEM((slots, PAD, width), F), pltpu.VMEM((2, blk, width), F),
             pltpu.VMEM((td * PAD, total * PAD), BF),
             pltpu.VMEM((nb, rb, rep), BF), pltpu.VMEM((nb, rb, rep), BF),
             pltpu.VMEM((rb, rep), BF), pltpu.VMEM((nb, rb, rep), BF),
             pltpu.VMEM((total, PAD, pc), BF), pltpu.VMEM((total, PAD, pc), BF),
             pltpu.VMEM((td * PAD, rep), F),
-            dma((7,)), dma((rows // blk,)), dma((nb,)), dma((nb,)), dma((nb,)), dma((nb,)), dma((total,)), dma((total,)),
+            dma((5,)), dma((3, slots)), dma((slots,)), dma((nb,)), dma((nb,)), dma((nb,)), dma((nb,)), dma((total,)),
+            dma((total,)),
         ],
         compiler_params=pltpu.CompilerParams(vmem_limit_bytes=62 * 2**20, collective_id=1, has_side_effects=True),
-        name="back",
-    )(task_ids, hid, gain, dpk.reshape(slots, PAD, width), dpv.reshape(slots, PAD, width),
-      outer, weight, dq, dk, dv, tokens, grad_mid)
+        name="back_attend",
+    )(task_ids, lengths, hid, gain, lse, pkv, outer, weight, qkv, attended, grad_att, tokens, grad_mid)
 
 
 def tail_kernel(plen, ig_in, emb_ref, inner_ref, gpre_ref, low_ref, gtl_ref,
@@ -752,12 +767,9 @@
     output, grad_mid, grad_attended = middle(
         second_gain, second_bias, tokens, attended, output_cotangent, output_weight, expand_weight, contract_weight
     )
-    grad_q, grad_k, grad_v, grad_pk, grad_pv = attn_bwd(
-        lengths, projected, prefix_kv, attended, grad_attended, log_totals, prefix_len
-    )
     input_grad, grad_pre, grad_table = back(
-        task_count, batch_count, ids, hidden_chunk, first_gain, grad_pk, grad_pv, reparam_outer, input_weight,
-        grad_q, grad_k, grad_v, tokens, grad_mid,
+        task_count, batch_count, ids, lengths, hidden_chunk, first_gain, log_totals, prefix_kv, reparam_outer,
+        input_weight, projected, attended, grad_attended, tokens, grad_mid, prefix_len,
     )
     input_grad, grad_embed, grad_inner, grad_inner_bias, grad_outer, grad_outer_bias = tail(
         input_grad, embed, reparam_inner, grad_pre, hidden_low, grad_table

time: 168 us -> 158 us (0.940)
  Pallas kernels: 167 us -> 157 us
    pallas_call x2 -> x1, Pallas kernels: 64.8 us -> 55.1 us  [back(): pl.pallas_call(functools.partial(back_kernel, nt, nb, td, plen, blk), in_...]
where the time goes in v2:
time: 158 us
  Pallas kernels  157 us (99%)
    pallas_call x1, Pallas kernels, back(): pl.pallas_call(functools.partial(back_kernel, nt, nb, td, plen, blk), in_...  55.1 us
    pallas_call x1, Pallas kernels, middle(): pl.pallas_call(functools.partial(middle_kernel, blk, fch), in_specs=[vm,...  49.9 us
    pallas_call x1, Pallas kernels, front(): pl.pallas_call(functools.partial(front_kernel, nt, nb, td, plen, chunk),...  42.4 us
    pallas_call x1, Pallas kernels, tail(): pl.pallas_call(functools.partial(tail_kernel, plen), grid=(td // per,), i...  9.71 us

profile of v2, /device:TPU:0, one launch (start us, length us, event | category | flops | bytes accessed | tf_op | source)
XLA Modules:
  0.0 157.8 jit_solution(385184739989069911)
XLA Ops:
  0.6 42.4 %front_attend.1 = (bf16[1024,3072]{1,0:T(8,128)(2,1)}, bf16[1024,1024]{1,0:T(8,128)(2,1)}, bf16[64,2048]{1,0:T(8,128)(2,1)}, f32[32,512]{1,0:T(8,128)}, bf16[256,512]{1,0:T(8,128)(2,1)}, /*index=5*/f32[8,2,1024]{2,1,0:T(2,128)}) custom-call(s32[4,32]{1,0:T(4,128)} %bitcast.7, s32[1,4]{1,0:T(1,128)} %len_ref.3, bf16[10,16,128]{2,1,0:T(8,128)(2,1)} %bitcast.5, ...), custom_call_target="tpu_custom_call" | custom-call | tf_op jit(solution)/shard_map/front_attend/pallas_call | solution.py:283
  43.0 49.9 %middle.1 = (bf16[1024,1024]{1,0:T(8,128)(2,1)}, f32[1024,1024]{1,0:T(8,128)}, bf16[1024,1024]{1,0:T(8,128)(2,1)}) custom-call(bf16[1024]{0:T(1024)(128)(2,1)} %g_ref.4, bf16[1024]{0:T(1024)(128)(2,1)} %b_ref.3, bf16[1024,1024]{1,0:T(8,128)(2,1)} %tok_hbm.5, bf16[1024,1024]{1,0:T(8,128)(2,1)} %get-tuple-element.25.att_hbm, bf16[1024,1024]{1,0:T(8,128)(2,1)} %ct_hbm.1, ...), custom_call_target="tpu_custom_call" | custom-call | tf_op jit(solution)/shard_map/middle/pallas_call | solution.py:392
  93.0 55.1 %back_attend.1 = (bf16[1024,1024]{1,0:T(8,128)(2,1)}, bf16[256,512]{1,0:T(8,128)(2,1)}, bf16[256,256]{1,0:T(8,128)(2,1)}) custom-call(s32[4,32]{1,0:T(4,128)} %bitcast.8, s32[1,4]{1,0:T(1,128)} %len_ref.3, f32[32,512]{1,0:T(8,128)} %get-tuple-element.27.hid_ref, bf16[1024]{0:T(1024)(128)(2,1)} %g_ref.5, f32[8,2,1024]{2,1,0:T(2,128)} %get-tuple-element.28.lse_ref, ...), custom_call_target="tpu_custom_call" | custom-call | tf_op jit(solution)/shard_map/back_attend/pallas_call | solution.py:668
  148.1 9.7 %tail.1 = (bf16[1024,1024]{1,0:T(8,128)(2,1)}, f32[160,128]{1,0:T(8,128)}, f32[16,128,512]{2,1,0:T(8,128)}, f32[16,512]{1,0:T(8,128)}, f32[16,512,256]{2,1,0:T(8,128)}, /*index=5*/f32[16,256]{1,0:T(8,128)}) custom-call(bf16[1024,1024]{1,0:T(8,128)(2,1)} %get-tuple-element.33.ig_in, bf16[10,16,128]{2,1,0:T(8,128)(2,1)} %bitcast.6, ...), custom_call_target="tpu_custom_call" | custom-call | tf_op jit(solution)/shard_map/tail/pallas_call | solution.py:726

commit v3 on v2

--- a/solution.py
+++ b/solution.py
@@ -16,6 +16,9 @@
 
 def dg(a, b, ca, cb):
     return lax.dot_general(a, b, (((ca,), (cb,)), ((), ())), preferred_element_type=F)
+
+
+AHEAD = 3
 
 
 def peer_id(flat, nb):
@@ -174,39 +177,44 @@
     tri = lax.broadcasted_iota(jnp.int32, (blk, blk), 0) <= lax.broadcasted_iota(jnp.int32, (blk, blk), 1)
 
     def attend(h, c):
-        pl.when(h == 1)(send_table)
+        pl.when(h == 2)(send_table)
         part = lambda third: qkv[:, pl.ds(pl.multiple_of(third * width + h * pair, pair), pair)]
         q_all = part(0) * jnp.asarray(scale, BF)
         k = part(1)
         km[0] = jnp.where(first, k, zero)
         km[1] = jnp.where(first, zero, k)
         vt = part(2).T
-
-        def scores(i):
-            q = q_all[i * blk:(i + 1) * blk]
-            return [dg(km[j, 0:(i + 1) * blk, :], q, 1, 1) for j in range(2)]
-
-        nxt = scores(0)
-        for i in range(slots):
+        ones = jnp.ones((PAD, rows), BF)
+        vts = [jnp.concatenate([vt[j * hd:(j + 1) * hd], ones], axis=0) for j in range(2)]
+        items = [(i, j) for i in range(slots) for j in range(2)]
+
+        def scores(n):
+            i, j = items[n]
+            return dg(km[j, 0:(i + 1) * blk, :], q_all[i * blk:(i + 1) * blk], 1, 1)
+
+        def top_of(n, s):
+            lo = items[n][0] * blk
+            top = jnp.max(jnp.where(tri, s[lo:], NEG), axis=0, keepdims=True)
+            if lo:
+                top = jnp.maximum(top, jnp.where(single, jnp.max(s[:lo], axis=0, keepdims=True), NEG))
+            return top
+
+        ahead = [scores(n) for n in range(AHEAD)]
+        nxt_top = top_of(0, ahead[0])
+        for n, (i, j) in enumerate(items):
             lo, hi = i * blk, (i + 1) * blk
-            cur = nxt
-            if i + 1 < slots:
-                nxt = scores(i + 1)
-            for j, s in enumerate(cur):
-                s_dia = jnp.where(tri, s[lo:], NEG)
-                top = jnp.max(s_dia, axis=0, keepdims=True)
-                if i:
-                    top = jnp.maximum(top, jnp.where(single, jnp.max(s[:lo], axis=0, keepdims=True), NEG))
-                p = jnp.exp(s_dia - top)
-                tot = jnp.sum(p, axis=0, keepdims=True)
-                p = p.astype(BF)
-                if i:
-                    p_off = jnp.exp(s[:lo] - jnp.where(single, top, -NEG))
-                    tot = tot + jnp.sum(p_off, axis=0, keepdims=True)
-                    p = jnp.concatenate([p_off.astype(BF), p], axis=0)
-                ot_s[pl.ds(pl.multiple_of(h * pair + j * hd, hd), hd), lo:hi] = dg(vt[j * hd:(j + 1) * hd, 0:hi], p, 1, 0)
-                top_s[h, j:j + 1, lo:hi] = top
-                sum_s[h, j:j + 1, lo:hi] = tot
+            s, top = ahead.pop(0), nxt_top
+            if n + AHEAD < len(items):
+                ahead.append(scores(n + AHEAD))
+            if n + 1 < len(items):
+                nxt_top = top_of(n + 1, ahead[0])
+            p = jnp.exp(jnp.where(tri, s[lo:], NEG) - top).astype(BF)
+            if i:
+                p = jnp.concatenate([jnp.exp(s[:lo] - jnp.where(single, top, -NEG)).astype(BF), p], axis=0)
+            ot = dg(vts[j][:, 0:hi], p, 1, 0)
+            ot_s[pl.ds(pl.multiple_of(h * pair + j * hd, hd), hd), lo:hi] = ot[:hd]
+            top_s[h, j:j + 1, lo:hi] = top
+            sum_s[h, j:j + 1, lo:hi] = ot[hd:hd + 1]
         return c
 
     lax.fori_loop(0, pairs, attend, 0)
@@ -572,12 +580,12 @@
             return dg(km[j, 0:hi, :], q_all[lo:hi], 1, 1), dg(vm[j, 0:hi, :], do_all[lo:hi], 1, 1)
 
         items = [(i, j) for i in range(slots) for j in range(2)]
-        nxt = scores(*items[0])
+        ahead = [scores(*items[n]) for n in range(2)]
         for n, (i, j) in enumerate(items):
             lo, hi = i * blk, (i + 1) * blk
-            s, dp = nxt
-            if n + 1 < len(items):
-                nxt = scores(*items[n + 1])
+            s, dp = ahead.pop(0)
+            if n + 2 < len(items):
+                ahead.append(scores(*items[n + 2]))
             lse = lse_ref[h, j:j + 1, lo:hi]
             delta = del_s[h, j:j + 1, lo:hi]
             p = jnp.where(tri, jnp.exp(s[lo:] - lse), 0.0)
@@ -689,51 +697,79 @@
     )(task_ids, lengths, hid, gain, lse, pkv, outer, weight, qkv, attended, grad_att, tokens, grad_mid)
 
 
-def tail_kernel(plen, ig_in, emb_ref, inner_ref, gpre_ref, low_ref, gtl_ref,
-                ig_out, ge_ref, gi_ref, gib_ref, go_ref, gob_ref, emf):
-    step = pl.program_id(0)
-    ig_out[...] = ig_in[...]
-
-    @pl.when(step == 0)
-    def _():
-        emf[...] = emb_ref[...].astype(F).reshape(emf.shape)
-
-    per = inner_ref.shape[0]
+def tail_kernel(plen, emb_ref, gpre_ref, low_ref, gtl_ref, ig_in, inner_hbm,
+                ge_ref, gib_ref, gob_ref, ig_out, gi_hbm, go_hbm,
+                ig, inner, gi, go, emf, embp, embt, lowt, ld_sem, ig_sem, gi_sem, go_sem):
     td = gib_ref.shape[0]
-    for k in range(per):
-        r = slice(k * PAD, (k + 1) * PAD)
-        gp = gpre_ref[r, :]
-        gt = gtl_ref[r, :]
-        at = pl.ds(step * per + k, 1)
-        spread = pl.ds(step * per + k, plen, stride=td)
-        gi_ref[k] = dg(emf[spread, :].astype(BF), gp[0:plen], 0, 0)
-        go_ref[k] = dg(low_ref[r, :], gt, 0, 0)
-        ge_ref[spread, :] = dg(gp, inner_ref[k], 1, 1)[0:plen]
-        gib_ref[at, :] = jnp.sum(gp[0:plen].astype(F), axis=0, keepdims=True)
-        gob_ref[at, :] = jnp.sum(gt[0:plen].astype(F), axis=0, keepdims=True)
+    ig_load = pltpu.make_async_copy(ig_in, ig, ld_sem.at[0])
+    in_load = pltpu.make_async_copy(inner_hbm, inner, ld_sem.at[1])
+    ig_load.start()
+    in_load.start()
+    emf[...] = emb_ref[...].astype(F).reshape(emf.shape)
+    embp[...] = jnp.zeros_like(embp)
+    for t in range(td):
+        embp[t * PAD:t * PAD + plen, :] = emf[pl.ds(t, plen, stride=td), :]
+    embt[...] = embp[...].astype(BF).T
+    lowt[...] = low_ref[...].T
+    zero = jnp.zeros((), BF)
+
+    def stores(t):
+        return [pltpu.make_async_copy(go.at[t], go_hbm.at[t], go_sem.at[t]),
+                pltpu.make_async_copy(gi.at[t], gi_hbm.at[t], gi_sem.at[t])]
+
+    def step(t, c):
+        only = lambda x: jnp.where(lax.broadcasted_iota(jnp.int32, x.shape, 0) // PAD == t, x, zero)
+        go[t] = dg(lowt[...], only(gtl_ref[...]), 1, 0)
+        gi[t] = dg(embt[...], only(gpre_ref[...]), 1, 0)
+        for cp in stores(t):
+            cp.start()
+        return c
+
+    lax.fori_loop(0, td // 2, step, 0)
+    ig_load.wait()
+    ig_store = pltpu.make_async_copy(ig, ig_out, ig_sem)
+    ig_store.start()
+    lax.fori_loop(td // 2, td, step, 0)
+    in_load.wait()
+    for t in range(td):
+        ge_ref[pl.ds(t, plen, stride=td), :] = dg(gpre_ref[t * PAD:(t + 1) * PAD, :], inner[t], 1, 1)[0:plen]
+    shape = (td, td * PAD)
+    own = lax.broadcasted_iota(jnp.int32, shape, 0) == lax.broadcasted_iota(jnp.int32, shape, 1) // PAD
+    picker = jnp.where(own, 1.0, 0.0).astype(BF)
+    gib_ref[...] = dg(picker, gpre_ref[...], 1, 0)
+    gob_ref[...] = dg(picker, gtl_ref[...], 1, 0)
+
+    def wait_step(t, c):
+        for cp in stores(t):
+            cp.wait()
+        return c
+
+    lax.fori_loop(0, td, wait_step, 0)
+    ig_store.wait()
 
 
 def tail(ig, emb, inner, gpre, low, gtl):
     plen, td, depth = emb.shape
     rep = inner.shape[2]
     pc = gtl.shape[1]
-    per = 2
     sds = jax.ShapeDtypeStruct
-    rows = pl.BlockSpec((ig.shape[0] * per // td, ig.shape[1]), lambda i: (i, 0))
-    lead = lambda *shape: pl.BlockSpec((per,) + shape, lambda i: (i,) + (0,) * len(shape))
-    flat = lambda cols: pl.BlockSpec((per * PAD, cols), lambda i: (i, 0))
-    full = lambda cols: pl.BlockSpec((td, cols), lambda i: (0, 0))
-    return pl.pallas_call(
+    vm = pl.BlockSpec(memory_space=pltpu.VMEM)
+    hb = pl.BlockSpec(memory_space=pl.ANY)
+    dma = pltpu.SemaphoreType.DMA
+    ge, gib, gob, ig, gi, go = pl.pallas_call(
         functools.partial(tail_kernel, plen),
-        grid=(td // per,),
-        in_specs=[rows, pl.BlockSpec((plen, td, depth), lambda i: (0, 0, 0)), lead(depth, rep), flat(rep), flat(rep), flat(pc)],
-        out_specs=[rows, pl.BlockSpec((plen * td, depth), lambda i: (0, 0)), lead(depth, rep), full(rep), lead(rep, pc), full(pc)],
-        out_shape=[sds(ig.shape, BF), sds((plen * td, depth), F), sds((td, depth, rep), F), sds((td, rep), F),
-                   sds((td, rep, pc), F), sds((td, pc), F)],
-        scratch_shapes=[pltpu.VMEM((plen * td, depth), F)],
+        in_specs=[vm, vm, vm, vm, hb, hb],
+        out_specs=[vm, vm, vm, hb, hb, hb],
+        out_shape=[sds((plen * td, depth), F), sds((td, rep), F), sds((td, pc), F), sds(ig.shape, BF),
+                   sds((td, depth, rep), F), sds((td, rep, pc), F)],
+        scratch_shapes=[pltpu.VMEM(ig.shape, BF), pltpu.VMEM(inner.shape, BF), pltpu.VMEM((td, depth, rep), F),
+                        pltpu.VMEM((td, rep, pc), F), pltpu.VMEM((plen * td, depth), F), pltpu.VMEM((td * PAD, depth), F),
+                        pltpu.VMEM((depth, td * PAD), BF), pltpu.VMEM((rep, td * PAD), BF),
+                        dma((2,)), dma, dma((td,)), dma((td,))],
         compiler_params=pltpu.CompilerParams(vmem_limit_bytes=62 * 2**20),
         name="tail",
-    )(ig, emb, inner, gpre, low, gtl)
+    )(emb, gpre, low, gtl, ig, inner)
+    return ig, ge, gi, gib, go, gob
 
 
 def local(

time: 158 us -> 153 us (0.968)
  Pallas kernels: 157 us -> 152 us
    pallas_call x1, Pallas kernels: 42.4 us -> 40 us  [front(): pl.pallas_call(functools.partial(front_kernel, nt, nb, td, plen, chunk),...]
    pallas_call x1, Pallas kernels: 9.71 us -> 8.03 us  [tail(): pl.pallas_call(functools.partial(tail_kernel, plen), in_specs=[vm, vm, vm...]
where the time goes in v3:
time: 153 us
  Pallas kernels  152 us (99%)
    pallas_call x1, Pallas kernels, back(): pl.pallas_call(functools.partial(back_kernel, nt, nb, td, plen, blk), in_...  54.4 us
    pallas_call x1, Pallas kernels, middle(): pl.pallas_call(functools.partial(middle_kernel, blk, fch), in_specs=[vm,...  49.9 us
    pallas_call x1, Pallas kernels, front(): pl.pallas_call(functools.partial(front_kernel, nt, nb, td, plen, chunk),...  40 us
    pallas_call x1, Pallas kernels, tail(): pl.pallas_call(functools.partial(tail_kernel, plen), in_specs=[vm, vm, vm...  8.03 us

profile of v3, /device:TPU:0, one launch (start us, length us, event | category | flops | bytes accessed | tf_op | source)
XLA Modules:
  0.0 153.2 jit_solution(7473231486702568769)
XLA Ops:
  0.6 40.0 %front_attend.1 = (bf16[1024,3072]{1,0:T(8,128)(2,1)}, bf16[1024,1024]{1,0:T(8,128)(2,1)}, bf16[64,2048]{1,0:T(8,128)(2,1)}, f32[32,512]{1,0:T(8,128)}, bf16[256,512]{1,0:T(8,128)(2,1)}, /*index=5*/f32[8,2,1024]{2,1,0:T(2,128)}) custom-call(s32[4,32]{1,0:T(4,128)} %bitcast.7, s32[1,4]{1,0:T(1,128)} %len_ref.3, bf16[10,16,128]{2,1,0:T(8,128)(2,1)} %bitcast.5, ...), custom_call_target="tpu_custom_call" | custom-call | tf_op jit(solution)/shard_map/front_attend/pallas_call | solution.py:291
  40.7 49.9 %middle.1 = (bf16[1024,1024]{1,0:T(8,128)(2,1)}, f32[1024,1024]{1,0:T(8,128)}, bf16[1024,1024]{1,0:T(8,128)(2,1)}) custom-call(bf16[1024]{0:T(1024)(128)(2,1)} %g_ref.4, bf16[1024]{0:T(1024)(128)(2,1)} %b_ref.3, bf16[1024,1024]{1,0:T(8,128)(2,1)} %tok_hbm.5, bf16[1024,1024]{1,0:T(8,128)(2,1)} %get-tuple-element.25.att_hbm, bf16[1024,1024]{1,0:T(8,128)(2,1)} %ct_hbm.1, ...), custom_call_target="tpu_custom_call" | custom-call | tf_op jit(solution)/shard_map/middle/pallas_call | solution.py:400
  90.6 54.4 %back_attend.1 = (bf16[1024,1024]{1,0:T(8,128)(2,1)}, bf16[256,512]{1,0:T(8,128)(2,1)}, bf16[256,256]{1,0:T(8,128)(2,1)}) custom-call(s32[4,32]{1,0:T(4,128)} %bitcast.8, s32[1,4]{1,0:T(1,128)} %len_ref.3, f32[32,512]{1,0:T(8,128)} %get-tuple-element.27.hid_ref, bf16[1024]{0:T(1024)(128)(2,1)} %g_ref.5, f32[8,2,1024]{2,1,0:T(2,128)} %get-tuple-element.28.lse_ref, ...), custom_call_target="tpu_custom_call" | custom-call | tf_op jit(solution)/shard_map/back_attend/pallas_call | solution.py:676
  145.0 8.0 %tail.1 = (f32[160,128]{1,0:T(8,128)}, f32[16,512]{1,0:T(8,128)}, f32[16,256]{1,0:T(8,128)}, bf16[1024,1024]{1,0:T(8,128)(2,1)}, f32[16,128,512]{2,1,0:T(8,128)}, /*index=5*/f32[16,512,256]{2,1,0:T(8,128)}) custom-call(bf16[10,16,128]{2,1,0:T(8,128)(2,1)} %bitcast.6, bf16[256,512]{1,0:T(8,128)(2,1)} %get-tuple-element.33.gpre_ref, ...), custom_call_target="tpu_custom_call" | custom-call | tf_op jit(solution)/shard_map/tail/pallas_call | solution.py:759

commit v4 on v3

--- a/solution.py
+++ b/solution.py
@@ -19,6 +19,7 @@
 
 
 AHEAD = 3
+PARTS = 4
 
 
 def peer_id(flat, nb):
@@ -46,6 +47,15 @@
     return barrier, me, total
 
 
+def strip_rows(slots, blk):
+    at = [blk * i * (i + 1) for i in range(slots + 1)]
+    return at, at[-1]
+
+
+def strip_parts(total):
+    return [slice(n * total // PARTS, (n + 1) * total // PARTS) for n in range(PARTS)]
+
+
 def spread_heads(block, heads, hd):
     wide = jnp.concatenate([block] * heads, axis=0)
     row = lax.broadcasted_iota(jnp.int32, wide.shape, 0) // PAD
@@ -60,9 +70,9 @@
 
 def front_kernel(nt, nb, td, plen, chunk,
                  ids_ref, len_ref, emb_ref, ib_ref, ob_ref, g_ref, b_ref, tok_hbm, w_hbm, inner_hbm, outer_hbm,
-                 qkv_hbm, att_hbm, pkv_ref, hid_ref, low_ref, lse_ref,
-                 tok, w, inner, outer, normed, qkv, ot_s, km, top_s, sum_s, pre, emf, ibf, tbl, rs_out, rs_in, ag_out, ag_in, aa_out, aa_in,
-                 ld_sem, st_sem, at_sem, rs_ss, rs_rs, ag_ss, ag_rs, aa_ss, aa_rs):
+                 qkv_hbm, att_hbm, p_hbm, pkv_ref, hid_ref, low_ref, lse_ref, fac_ref,
+                 tok, w, inner, outer, normed, qkv, ot_s, km, p_s, top_s, sum_s, pre, emf, ibf, tbl, rs_out, rs_in, ag_out, ag_in, aa_out, aa_in,
+                 ld_sem, st_sem, at_sem, p_sem, rs_ss, rs_rs, ag_ss, ag_rs, aa_ss, aa_rs):
     rows, width = tok.shape
     slots = ids_ref.shape[0]
     rc = td * PAD // nb
@@ -71,12 +81,14 @@
     mb = lax.axis_index("batch")
     loads = [pltpu.make_async_copy(s, d, ld_sem.at[i])
              for i, (s, d) in enumerate(((inner_hbm, inner), (tok_hbm, tok), (w_hbm, w), (outer_hbm, outer)))]
-    for c in loads:
+    for c in loads[:2]:
         c.start()
     barrier, me, total = greet_all(nt, nb)
     pre[...] = jnp.zeros_like(pre)
     emf[...] = emb_ref[...].astype(F).reshape(emf.shape)
     loads[0].wait()
+    for c in loads[2:]:
+        c.start()
     for t in range(td):
         pre[t * PAD:t * PAD + plen, :] = dg(emf[pl.ds(t, plen, stride=td), :].astype(BF), inner[t], 1, 0)
     for c in range(nb):
@@ -176,8 +188,21 @@
     zero = jnp.zeros((), BF)
     tri = lax.broadcasted_iota(jnp.int32, (blk, blk), 0) <= lax.broadcasted_iota(jnp.int32, (blk, blk), 1)
 
+    at_row, p_rows = strip_rows(slots, blk)
+
+    def p_copies(h):
+        buf = lax.rem(h, 2)
+        return [pltpu.make_async_copy(p_s.at[buf, r], p_hbm.at[h, r], p_sem.at[buf, n])
+                for n, r in enumerate(strip_parts(p_rows))]
+
+    def p_wait(h):
+        for cp in p_copies(h):
+            cp.wait()
+
     def attend(h, c):
         pl.when(h == 2)(send_table)
+        pl.when(h >= 2)(lambda: p_wait(h - 2))
+        buf = lax.rem(h, 2)
         part = lambda third: qkv[:, pl.ds(pl.multiple_of(third * width + h * pair, pair), pair)]
         q_all = part(0) * jnp.asarray(scale, BF)
         k = part(1)
@@ -211,10 +236,13 @@
             p = jnp.exp(jnp.where(tri, s[lo:], NEG) - top).astype(BF)
             if i:
                 p = jnp.concatenate([jnp.exp(s[:lo] - jnp.where(single, top, -NEG)).astype(BF), p], axis=0)
+            p_s[buf, at_row[i] + j * hi:at_row[i] + (j + 1) * hi, :] = p
             ot = dg(vts[j][:, 0:hi], p, 1, 0)
             ot_s[pl.ds(pl.multiple_of(h * pair + j * hd, hd), hd), lo:hi] = ot[:hd]
             top_s[h, j:j + 1, lo:hi] = top
             sum_s[h, j:j + 1, lo:hi] = ot[hd:hd + 1]
+        for cp in p_copies(h):
+            cp.start()
         return c
 
     lax.fori_loop(0, pairs, attend, 0)
@@ -255,6 +283,7 @@
             inv = 1.0 / tot
             ps.append(p.astype(BF))
             alphas.append(alpha * inv)
+            fac_ref[hh // 2, hh % 2:hh % 2 + 1, cols] = alpha * inv
             invs.append(inv)
         vt = spread(prefix_rows(pkv_ref, single, i, width, 2 * width)).T
         pre = dg(vt, jnp.concatenate(ps, axis=0), 1, 0)
@@ -269,6 +298,8 @@
         c.wait_send()
     for j in range(steps):
         store(j).wait()
+    p_wait(pairs - 2)
+    p_wait(pairs - 1)
     for i in range(slots):
         att_store(i).wait()
 
@@ -284,6 +315,7 @@
     rb = max(rc, PAD)
     chunk = 1024
     steps = weight.shape[1] // chunk
+    p_rows = strip_rows(slots, rows // slots)[1]
     sds = jax.ShapeDtypeStruct
     vm = pl.BlockSpec(memory_space=pltpu.VMEM)
     hb = pl.BlockSpec(memory_space=pl.ANY)
@@ -291,19 +323,19 @@
     return pl.pallas_call(
         functools.partial(front_kernel, nt, nb, td, plen, chunk),
         in_specs=[pl.BlockSpec(memory_space=pltpu.SMEM)] * 2 + [vm] * 5 + [hb] * 4,
-        out_specs=[hb, hb, vm, vm, vm, vm],
-        out_shape=[sds((rows, weight.shape[1]), BF), sds((rows, width), BF), sds((slots * PAD, nb * pc), BF), sds((rc, rep), F),
-                   sds((td * PAD, rep), BF), sds((width // 128, 2, rows), F)],
+        out_specs=[hb, hb, hb, vm, vm, vm, vm, vm],
+        out_shape=[sds((rows, weight.shape[1]), BF), sds((rows, width), BF), sds((width // 128, p_rows, rows // slots), BF), sds((slots * PAD, nb * pc), BF), sds((rc, rep), F),
+                   sds((td * PAD, rep), BF), sds((width // 128, 2, rows), F), sds((width // 128, 2, rows), F)],
         scratch_shapes=[
             pltpu.VMEM((rows, width), BF), pltpu.VMEM(weight.shape, BF), pltpu.VMEM(inner.shape, BF),
             pltpu.VMEM(outer.shape, BF), pltpu.VMEM((rows, width), BF), pltpu.VMEM((rows, weight.shape[1]), BF),
-            pltpu.VMEM((width, rows), F), pltpu.VMEM((2, rows, 128), BF),
+            pltpu.VMEM((width, rows), F), pltpu.VMEM((2, rows, 128), BF), pltpu.VMEM((2, p_rows, rows // slots), BF),
             pltpu.VMEM((width // 128, 2, rows), F), pltpu.VMEM((width // 128, 2, rows), F),
             pltpu.VMEM((td * PAD, rep), F), pltpu.VMEM((plen * td, depth), F), pltpu.VMEM((td * PAD, rep), F), pltpu.VMEM((td, PAD, pc), BF),
             pltpu.VMEM((nb, rb, rep), BF), pltpu.VMEM((nb, rb, rep), BF),
             pltpu.VMEM((rb, rep), BF), pltpu.VMEM((nb, rb, rep), BF),
             pltpu.VMEM((total, PAD, pc), BF), pltpu.VMEM((total, PAD, pc), BF),
-            dma((4,)), dma((steps,)), dma((slots,)), dma((nb,)), dma((nb,)), dma((nb,)), dma((nb,)), dma((total,)), dma((total,)),
+            dma((4,)), dma((steps,)), dma((slots,)), dma((2, PARTS)), dma((nb,)), dma((nb,)), dma((nb,)), dma((nb,)), dma((total,)), dma((total,)),
         ],
         compiler_params=pltpu.CompilerParams(vmem_limit_bytes=62 * 2**20, collective_id=0, has_side_effects=True),
         name="front_attend",
@@ -411,12 +443,12 @@
 
 
 def back_kernel(nt, nb, td, plen, blk,
-                ids_ref, len_ref, hid_ref, g_ref, lse_ref, pkv_ref, outer_hbm, w_hbm, qkv_hbm, att_hbm, do_hbm, tok_hbm,
-                gm_hbm,
+                ids_ref, len_ref, hid_ref, g_ref, lse_ref, fac_ref, pkv_ref, outer_hbm, w_hbm, qkv_hbm, att_hbm, do_hbm, tok_hbm,
+                gm_hbm, p_hbm,
                 ig_hbm, gpre_ref, gtl_ref,
-                outer, w, qkv, att, do_s, tok, gm, dqkv, dqp, km, vm, dka, dva, del_s, dpk_s, dpv_s, gbuf,
+                outer, w, qkv, att, do_s, tok, gm, dqkv, dqp, p_s, vm, dka, dva, del_s, dpk_s, dpv_s, gbuf,
                 sel, rs_out, rs_in, ag_out, ag_in, aa_out, aa_in, part,
-                ld_sem, bl_sem, st_sem, rs_ss, rs_rs, ag_ss, ag_rs, aa_ss, aa_rs):
+                ld_sem, bl_sem, p_sem, st_sem, rs_ss, rs_rs, ag_ss, ag_rs, aa_ss, aa_rs):
     rows, width = tok.shape
     slots = ids_ref.shape[0]
     rc = td * PAD // nb
@@ -445,8 +477,13 @@
     for i in range(slots):
         for c in block_loads(i):
             c.start()
-    for c in loads:
-        c.start()
+    at_row, p_rows = strip_rows(slots, blk)
+
+    def p_copies(h):
+        buf = lax.rem(h, 2)
+        return [pltpu.make_async_copy(p_hbm.at[h, r], p_s.at[buf, r], p_sem.at[buf, n])
+                for n, r in enumerate(strip_parts(p_rows))]
+
     barrier, me, total = greet_all(nt, nb)
     live = lax.broadcasted_iota(jnp.int32, (PAD, blk), 0) < plen
     lane_head = lax.broadcasted_iota(jnp.int32, (heads, width), 1) // hd
@@ -458,6 +495,12 @@
         cols = rows_of(i)
         for cp in block_loads(i):
             cp.wait()
+
+        @pl.when(i == 1)
+        def _():
+            for cp in loads[:1] + p_copies(0) + p_copies(1):
+                cp.start()
+
         q = qkv[cols, 0:width] * jnp.asarray(scale, BF)
         do = do_s[cols, :]
         prod = do.astype(F) * att[cols, :].astype(F)
@@ -470,7 +513,7 @@
         ps, dss = [], []
         for hh in range(heads):
             one = slice(hh * PAD, (hh + 1) * PAD)
-            del_s[hh // 2, hh % 2:hh % 2 + 1, cols] = delta[hh:hh + 1]
+            del_s[hh // 2, hh % 2:hh % 2 + 1, cols] = delta[hh:hh + 1] * fac_ref[hh // 2, hh % 2:hh % 2 + 1, cols]
             pr = jnp.where(live, jnp.exp(sp[one] - lse_ref[hh // 2, hh % 2:hh % 2 + 1, cols]), 0.0)
             ps.append(pr.astype(BF))
             dss.append((pr * (dpp[one] - delta[hh:hh + 1])).astype(BF))
@@ -482,6 +525,8 @@
         return c
 
     lax.fori_loop(0, slots, prefix_step, 0)
+    for c in loads[1:]:
+        c.start()
     for ref in (dpk_s, dpv_s):
         whole = ref[0]
         for i in range(1, slots):
@@ -560,41 +605,35 @@
     first = lax.broadcasted_iota(jnp.int32, (1, pair), 1) < hd
     zero = jnp.zeros((), BF)
     split = lambda a: (jnp.where(first, a, zero), jnp.where(first, zero, a))
-    tri = lax.broadcasted_iota(jnp.int32, (blk, blk), 0) <= lax.broadcasted_iota(jnp.int32, (blk, blk), 1)
     add = lambda a, b: b if a is None else a + b
 
     def attend(h, c):
-        pl.when(h == 2)(sum_table)
-        pl.when(h == 5)(sum_hidden)
+        pl.when(h == 3)(sum_table)
+        pl.when(h == 6)(sum_hidden)
         cols_of = lambda third: pl.ds(pl.multiple_of(third * width + h * pair, pair), pair)
+        for cp in p_copies(h):
+            cp.wait()
+        buf = lax.rem(h, 2)
         q_all = qkv[:, cols_of(0)] * jnp.asarray(scale, BF)
-        do_all = do_s[:, cols_of(0)]
-        k = qkv[:, cols_of(1)]
-        km[0], km[1] = split(k)
         vm[0], vm[1] = split(qkv[:, cols_of(2)])
-        kt = k.T
+        kt = qkv[:, cols_of(1)].T
+        fac = jnp.concatenate([jnp.broadcast_to(fac_ref[h, j:j + 1, :], (hd, rows)) for j in range(2)], axis=0).T
+        do_all = (do_s[:, cols_of(0)].astype(F) * fac).astype(BF)
         qs, dos = split(q_all), split(do_all)
 
         def scores(i, j):
             lo, hi = i * blk, (i + 1) * blk
-            return dg(km[j, 0:hi, :], q_all[lo:hi], 1, 1), dg(vm[j, 0:hi, :], do_all[lo:hi], 1, 1)
+            return dg(vm[j, 0:hi, :], do_all[lo:hi], 1, 1)
 
         items = [(i, j) for i in range(slots) for j in range(2)]
         ahead = [scores(*items[n]) for n in range(2)]
         for n, (i, j) in enumerate(items):
             lo, hi = i * blk, (i + 1) * blk
-            s, dp = ahead.pop(0)
+            dp = ahead.pop(0)
             if n + 2 < len(items):
                 ahead.append(scores(*items[n + 2]))
-            lse = lse_ref[h, j:j + 1, lo:hi]
-            delta = del_s[h, j:j + 1, lo:hi]
-            p = jnp.where(tri, jnp.exp(s[lo:] - lse), 0.0)
-            ds = (p * (dp[lo:] - delta)).astype(BF)
-            p = p.astype(BF)
-            if i:
-                off = jnp.exp(s[:lo] - jnp.where(single, lse, -NEG))
-                ds = jnp.concatenate([(off * (dp[:lo] - delta)).astype(BF), ds], axis=0)
-                p = jnp.concatenate([off.astype(BF), p], axis=0)
+            p = p_s[buf, at_row[i] + j * hi:at_row[i] + (j + 1) * hi, :]
+            ds = (p.astype(F) * (dp - del_s[h, j:j + 1, lo:hi])).astype(BF)
             if j == 0:
                 dk = dv = None
                 dqs = []
@@ -611,6 +650,12 @@
                     dva[0:lo, :] += dv[:lo]
         dqkv[:, cols_of(1)] = dka[...].astype(BF)
         dqkv[:, cols_of(2)] = dva[...].astype(BF)
+
+        @pl.when(h + 2 < pairs)
+        def _():
+            for cp in p_copies(h + 2):
+                cp.start()
+
         return c
 
     lax.fori_loop(0, pairs, attend, 0)
@@ -660,7 +705,8 @@
         store(i).wait()
 
 
-def back(nt, nb, task_ids, lengths, hid, gain, lse, pkv, outer, weight, qkv, attended, grad_att, tokens, grad_mid, plen):
+def back(nt, nb, task_ids, lengths, hid, gain, lse, fac, pkv, outer, weight, qkv, attended, grad_att, tokens, grad_mid,
+         lifted, plen):
     td, rep, pc = outer.shape
     rows, width = tokens.shape
     slots = task_ids.shape[0]
@@ -675,13 +721,13 @@
     full = lambda t: pltpu.VMEM((rows, width), t)
     return pl.pallas_call(
         functools.partial(back_kernel, nt, nb, td, plen, blk),
-        in_specs=[pl.BlockSpec(memory_space=pltpu.SMEM)] * 2 + [vm] * 4 + [hb] * 7,
+        in_specs=[pl.BlockSpec(memory_space=pltpu.SMEM)] * 2 + [vm] * 5 + [hb] * 8,
         out_specs=[hb, vm, vm],
         out_shape=[sds((rows, width), BF), sds((td * PAD, rep), BF), sds((td * PAD, pc), BF)],
         scratch_shapes=[
             pltpu.VMEM(outer.shape, BF), pltpu.VMEM(weight.shape, BF), pltpu.VMEM(qkv.shape, BF), full(BF), full(BF),
             full(BF), full(F), pltpu.VMEM(qkv.shape, BF), pltpu.VMEM((width, rows), F),
-            pltpu.VMEM((2, rows, 128), BF), pltpu.VMEM((2, rows, 128), BF), pltpu.VMEM((rows, 128), F),
+            pltpu.VMEM((2,) + lifted.shape[1:], BF), pltpu.VMEM((2, rows, 128), BF), pltpu.VMEM((rows, 128), F),
             pltpu.VMEM((rows, 128), F), pltpu.VMEM(lse.shape, F), pltpu.VMEM((slots, PAD, width), F),
             pltpu.VMEM((slots, PAD, width), F), pltpu.VMEM((2, blk, width), F),
             pltpu.VMEM((td * PAD, total * PAD), BF),
@@ -689,12 +735,12 @@
             pltpu.VMEM((rb, rep), BF), pltpu.VMEM((nb, rb, rep), BF),
             pltpu.VMEM((total, PAD, pc), BF), pltpu.VMEM((total, PAD, pc), BF),
             pltpu.VMEM((td * PAD, rep), F),
-            dma((5,)), dma((3, slots)), dma((slots,)), dma((nb,)), dma((nb,)), dma((nb,)), dma((nb,)), dma((total,)),
+            dma((5,)), dma((3, slots)), dma((2, PARTS)), dma((slots,)), dma((nb,)), dma((nb,)), dma((nb,)), dma((nb,)), dma((total,)),
             dma((total,)),
         ],
         compiler_params=pltpu.CompilerParams(vmem_limit_bytes=62 * 2**20, collective_id=1, has_side_effects=True),
         name="back_attend",
-    )(task_ids, lengths, hid, gain, lse, pkv, outer, weight, qkv, attended, grad_att, tokens, grad_mid)
+    )(task_ids, lengths, hid, gain, lse, fac, pkv, outer, weight, qkv, attended, grad_att, tokens, grad_mid, lifted)
 
 
 def tail_kernel(plen, emb_ref, gpre_ref, low_ref, gtl_ref, ig_in, inner_hbm,
@@ -796,7 +842,7 @@
     batch_count = lax.axis_size("batch")
     ids = task_ids.T
     embed = prefix_embed.transpose(1, 0, 2)
-    projected, attended, prefix_kv, hidden_chunk, hidden_low, log_totals = front(
+    projected, attended, lifted, prefix_kv, hidden_chunk, hidden_low, log_totals, factors = front(
         task_count, batch_count, ids, lengths, embed, reparam_inner, reparam_inner_bias, reparam_outer,
         reparam_outer_bias, first_gain, first_bias, tokens, input_weight,
     )
@@ -804,8 +850,8 @@
         second_gain, second_bias, tokens, attended, output_cotangent, output_weight, expand_weight, contract_weight
     )
     input_grad, grad_pre, grad_table = back(
-        task_count, batch_count, ids, lengths, hidden_chunk, first_gain, log_totals, prefix_kv, reparam_outer,
-        input_weight, projected, attended, grad_attended, tokens, grad_mid, prefix_len,
+        task_count, batch_count, ids, lengths, hidden_chunk, first_gain, log_totals, factors, prefix_kv, reparam_outer,
+        input_weight, projected, attended, grad_attended, tokens, grad_mid, lifted, prefix_len,
     )
     input_grad, grad_embed, grad_inner, grad_inner_bias, grad_outer, grad_outer_bias = tail(
         input_grad, embed, reparam_inner, grad_pre, hidden_low, grad_table

time: 153 us -> 148 us (0.967)
  Pallas kernels: 152 us -> 147 us
    pallas_call x1, Pallas kernels: 54.4 us -> 48.1 us  [back(): pl.pallas_call(functools.partial(back_kernel, nt, nb, td, plen, blk), in_...]
where the time goes in v4:
time: 148 us
  Pallas kernels  147 us (99%)
    pallas_call x1, Pallas kernels, middle(): pl.pallas_call(functools.partial(middle_kernel, blk, fch), in_specs=[vm,...  49.9 us
    pallas_call x1, Pallas kernels, back(): pl.pallas_call(functools.partial(back_kernel, nt, nb, td, plen, blk), in_...  48.1 us
    pallas_call x1, Pallas kernels, front(): pl.pallas_call(functools.partial(front_kernel, nt, nb, td, plen, chunk),...  40.9 us
    pallas_call x1, Pallas kernels, tail(): pl.pallas_call(functools.partial(tail_kernel, plen), in_specs=[vm, vm, vm...  8.03 us

profile of v4, /device:TPU:0, one launch (start us, length us, event | category | flops | bytes accessed | tf_op | source)
XLA Modules:
  0.0 147.7 jit_solution(15155628353379635082)
XLA Ops:
  0.6 40.9 %front_attend.1 = (bf16[1024,3072]{1,0:T(8,128)(2,1)}, bf16[1024,1024]{1,0:T(8,128)(2,1)}, bf16[8,5120,256]{2,1,0:T(8,128)(2,1)}, bf16[64,2048]{1,0:T(8,128)(2,1...) custom-call(s32[4,32]{1,0:T(4,128)} %bitcast.7, ...), custom_call_target="tpu_custom_call" | custom-call | tf_op jit(solution)/shard_map/front_attend/pallas_call | solution.py:323
  41.5 49.9 %middle.1 = (bf16[1024,1024]{1,0:T(8,128)(2,1)}, f32[1024,1024]{1,0:T(8,128)}, bf16[1024,1024]{1,0:T(8,128)(2,1)}) custom-call(bf16[1024]{0:T(1024)(128)(2,1)} %g_ref.4, bf16[1024]{0:T(1024)(128)(2,1)} %b_ref.3, bf16[1024,1024]{1,0:T(8,128)(2,1)} %tok_hbm.5, bf16[1024,1024]{1,0:T(8,128)(2,1)} %get-tuple-element.27.att_hbm, bf16[1024,1024]{1,0:T(8,128)(2,1)} %ct_hbm.1, ...), custom_call_target="tpu_custom_call" | custom-call | tf_op jit(solution)/shard_map/middle/pallas_call | solution.py:432
  91.5 48.1 %back_attend.1 = (bf16[1024,1024]{1,0:T(8,128)(2,1)}, bf16[256,512]{1,0:T(8,128)(2,1)}, bf16[256,256]{1,0:T(8,128)(2,1)}) custom-call(s32[4,32]{1,0:T(4,128)} %bitcast.8, s32[1,4]{1,0:T(1,128)} %len_ref.3, f32[32,512]{1,0:T(8,128)} %get-tuple-element.29.hid_ref, bf16[1024]{0:T(1024)(128)(2,1)} %g_ref.5, f32[8,2,1024]{2,1,0:T(2,128)} %get-tuple-element.30.lse_ref, ...), custom_call_target="tpu_custom_call" | custom-call | tf_op jit(solution)/shard_map/back_attend/pallas_call | solution.py:722
  139.5 8.0 %tail.1 = (f32[160,128]{1,0:T(8,128)}, f32[16,512]{1,0:T(8,128)}, f32[16,256]{1,0:T(8,128)}, bf16[1024,1024]{1,0:T(8,128)(2,1)}, f32[16,128,512]{2,1,0:T(8,128)}, /*index=5*/f32[16,512,256]{2,1,0:T(8,128)}) custom-call(bf16[10,16,128]{2,1,0:T(8,128)(2,1)} %bitcast.6, bf16[256,512]{1,0:T(8,128)(2,1)} %get-tuple-element.37.gpre_ref, ...), custom_call_target="tpu_custom_call" | custom-call | tf_op jit(solution)/shard_map/tail/pallas_call | solution.py:805

commit v5 on v4

--- a/solution.py
+++ b/solution.py
@@ -20,6 +20,7 @@
 
 AHEAD = 3
 PARTS = 4
+GROUP = 4
 
 
 def peer_id(flat, nb):
@@ -265,35 +266,42 @@
     def att_store(i):
         return pltpu.make_async_copy(normed.at[rows_of(i), :], att_hbm.at[rows_of(i), :], at_sem.at[i])
 
-    def merge(i, c):
-        cols = rows_of(i)
-        spread = lambda x: spread_heads(x, heads, hd)
-        q = qkv[cols, 0:width] * jnp.asarray(scale, BF)
-        sp = dg(spread(prefix_rows(pkv_ref, single, i, 0, width)), q, 1, 1)
-        live = lax.broadcasted_iota(jnp.int32, (PAD, blk), 0) < plen
-        ps, alphas, invs = [], [], []
-        for hh in range(heads):
-            s = jnp.where(live, sp[hh * PAD:(hh + 1) * PAD], NEG)
-            told = top_s[hh // 2, hh % 2:hh % 2 + 1, cols]
-            top = jnp.maximum(told, jnp.max(s, axis=0, keepdims=True))
-            p = jnp.exp(s - top)
-            alpha = jnp.exp(told - top)
-            tot = alpha * sum_s[hh // 2, hh % 2:hh % 2 + 1, cols] + jnp.sum(p, axis=0, keepdims=True)
-            lse_ref[hh // 2, hh % 2:hh % 2 + 1, cols] = top + jnp.log(tot)
-            inv = 1.0 / tot
-            ps.append(p.astype(BF))
-            alphas.append(alpha * inv)
-            fac_ref[hh // 2, hh % 2:hh % 2 + 1, cols] = alpha * inv
-            invs.append(inv)
-        vt = spread(prefix_rows(pkv_ref, single, i, width, 2 * width)).T
-        pre = dg(vt, jnp.concatenate(ps, axis=0), 1, 0)
-        outs = [ot_s[hh * hd:(hh + 1) * hd, cols] * alphas[hh] + pre[hh * hd:(hh + 1) * hd] * invs[hh]
-                for hh in range(heads)]
-        normed[cols, :] = jnp.concatenate(outs, axis=0).T.astype(BF)
-        att_store(i).start()
-        return c
-
-    lax.fori_loop(0, slots, merge, 0)
+    live = lax.broadcasted_iota(jnp.int32, (PAD, blk), 0) < plen
+    spread = lambda x: spread_heads(x, heads, hd)
+
+    def merge(g, c):
+        blocks = [g * GROUP + n for n in range(GROUP)]
+        sps = [dg(spread(prefix_rows(pkv_ref, single, i, 0, width)), qkv[rows_of(i), 0:width] * jnp.asarray(scale, BF), 1, 1)
+               for i in blocks]
+        vts = [spread(prefix_rows(pkv_ref, single, i, width, 2 * width)).T for i in blocks]
+        pres, alphas, invs = [], [], []
+        for i, sp, vt in zip(blocks, sps, vts):
+            cols = rows_of(i)
+            ps = []
+            for hh in range(heads):
+                at = (hh // 2, slice(hh % 2, hh % 2 + 1), cols)
+                s = jnp.where(live, sp[hh * PAD:(hh + 1) * PAD], NEG)
+                told = top_s[at]
+                top = jnp.maximum(told, jnp.max(s, axis=0, keepdims=True))
+                p = jnp.exp(s - top)
+                alpha = jnp.exp(told - top)
+                tot = alpha * sum_s[at] + jnp.sum(p, axis=0, keepdims=True)
+                lse_ref[at] = top + jnp.log(tot)
+                inv = 1.0 / tot
+                ps.append(p.astype(BF))
+                alphas.append(alpha * inv)
+                fac_ref[at] = alpha * inv
+                invs.append(inv)
+            pres.append(dg(vt, jnp.concatenate(ps, axis=0), 1, 0))
+        for n, i in enumerate(blocks):
+            cols = rows_of(i)
+            outs = [ot_s[hh * hd:(hh + 1) * hd, cols] * alphas[n * heads + hh]
+                    + pres[n][hh * hd:(hh + 1) * hd] * invs[n * heads + hh] for hh in range(heads)]
+            normed[cols, :] = jnp.concatenate(outs, axis=0).T.astype(BF)
+            att_store(i).start()
+        return c
+
+    lax.fori_loop(0, slots // GROUP, merge, 0)
     for c in rs_copy + ag_copy:
         c.wait_send()
     for j in range(steps):
@@ -491,40 +499,46 @@
     own_block = (lax.broadcasted_iota(jnp.int32, (heads * PAD, width), 0) // PAD
                  == lax.broadcasted_iota(jnp.int32, (heads * PAD, width), 1) // hd)
 
-    def prefix_step(i, c):
-        cols = rows_of(i)
-        for cp in block_loads(i):
-            cp.wait()
-
-        @pl.when(i == 1)
+    def prefix_step(g, c):
+        blocks = [g * GROUP + n for n in range(GROUP)]
+        for i in blocks:
+            for cp in block_loads(i):
+                cp.wait()
+
+        @pl.when(g == 0)
         def _():
             for cp in loads[:1] + p_copies(0) + p_copies(1):
                 cp.start()
 
-        q = qkv[cols, 0:width] * jnp.asarray(scale, BF)
-        do = do_s[cols, :]
-        prod = do.astype(F) * att[cols, :].astype(F)
-        high = prod.astype(BF)
-        delta = dg(picker, high, 1, 1) + dg(picker, (prod - high.astype(F)).astype(BF), 1, 1)
-        kp = spread_heads(prefix_rows(pkv_ref, single, i, 0, width), heads, hd)
-        vp = spread_heads(prefix_rows(pkv_ref, single, i, width, 2 * width), heads, hd)
-        sp = dg(kp, q, 1, 1)
-        dpp = dg(vp, do, 1, 1)
-        ps, dss = [], []
-        for hh in range(heads):
-            one = slice(hh * PAD, (hh + 1) * PAD)
-            del_s[hh // 2, hh % 2:hh % 2 + 1, cols] = delta[hh:hh + 1] * fac_ref[hh // 2, hh % 2:hh % 2 + 1, cols]
-            pr = jnp.where(live, jnp.exp(sp[one] - lse_ref[hh // 2, hh % 2:hh % 2 + 1, cols]), 0.0)
-            ps.append(pr.astype(BF))
-            dss.append((pr * (dpp[one] - delta[hh:hh + 1])).astype(BF))
-        ds = jnp.concatenate(dss, axis=0)
+        qs = [qkv[rows_of(i), 0:width] * jnp.asarray(scale, BF) for i in blocks]
+        dos = [do_s[rows_of(i), :] for i in blocks]
+        kps = [spread_heads(prefix_rows(pkv_ref, single, i, 0, width), heads, hd) for i in blocks]
+        sps = [dg(kp, q, 1, 1) for kp, q in zip(kps, qs)]
+        dpps = [dg(spread_heads(prefix_rows(pkv_ref, single, i, width, 2 * width), heads, hd), do, 1, 1)
+                for i, do in zip(blocks, dos)]
+        deltas = []
+        for i, do in zip(blocks, dos):
+            prod = do.astype(F) * att[rows_of(i), :].astype(F)
+            high = prod.astype(BF)
+            deltas.append(dg(picker, high, 1, 1) + dg(picker, (prod - high.astype(F)).astype(BF), 1, 1))
         fold = lambda x: jnp.sum(jnp.where(own_block, x, 0.0).reshape(heads, PAD, width), axis=0)
-        dpk_s[i] = fold(dg(ds, q, 1, 0))
-        dpv_s[i] = fold(dg(jnp.concatenate(ps, axis=0), do, 1, 0))
-        dqp[:, cols] = dg(kp.T, ds, 1, 0)
-        return c
-
-    lax.fori_loop(0, slots, prefix_step, 0)
+        for i, q, do, kp, sp, dpp, delta in zip(blocks, qs, dos, kps, sps, dpps, deltas):
+            cols = rows_of(i)
+            ps, dss = [], []
+            for hh in range(heads):
+                one = slice(hh * PAD, (hh + 1) * PAD)
+                at = (hh // 2, slice(hh % 2, hh % 2 + 1), cols)
+                del_s[at] = delta[hh:hh + 1] * fac_ref[at]
+                pr = jnp.where(live, jnp.exp(sp[one] - lse_ref[at]), 0.0)
+                ps.append(pr.astype(BF))
+                dss.append((pr * (dpp[one] - delta[hh:hh + 1])).astype(BF))
+            ds = jnp.concatenate(dss, axis=0)
+            dpk_s[i] = fold(dg(ds, q, 1, 0))
+            dpv_s[i] = fold(dg(jnp.concatenate(ps, axis=0), do, 1, 0))
+            dqp[:, cols] = dg(kp.T, ds, 1, 0)
+        return c
+
+    lax.fori_loop(0, slots // GROUP, prefix_step, 0)
     for c in loads[1:]:
         c.start()
     for ref in (dpk_s, dpv_s):
@@ -625,7 +639,7 @@
             lo, hi = i * blk, (i + 1) * blk
             return dg(vm[j, 0:hi, :], do_all[lo:hi], 1, 1)
 
-        items = [(i, j) for i in range(slots) for j in range(2)]
+        items = [(i, j) for i in reversed(range(slots)) for j in range(2)]
         ahead = [scores(*items[n]) for n in range(2)]
         for n, (i, j) in enumerate(items):
             lo, hi = i * blk, (i + 1) * blk
@@ -643,11 +657,12 @@
             if j:
                 dqt = jnp.concatenate(dqs, axis=0) + dqp[pl.ds(pl.multiple_of(h * pair, pair), pair), lo:hi]
                 dqkv[lo:hi, cols_of(0)] = (dqt.T * scale).astype(BF)
-                dka[lo:hi, :] = dk[lo:]
-                dva[lo:hi, :] = dv[lo:]
-                if i:
-                    dka[0:lo, :] += dk[:lo]
-                    dva[0:lo, :] += dv[:lo]
+                if i == slots - 1:
+                    dka[...] = dk
+                    dva[...] = dv
+                else:
+                    dka[0:hi, :] += dk
+                    dva[0:hi, :] += dv
         dqkv[:, cols_of(1)] = dka[...].astype(BF)
         dqkv[:, cols_of(2)] = dva[...].astype(BF)
 

time: 148 us -> 146 us (0.986)
  Pallas kernels: 147 us -> 145 us
    pallas_call x1, Pallas kernels: 40.9 us -> 39.1 us  [front(): pl.pallas_call(functools.partial(front_kernel, nt, nb, td, plen, chunk),...]
where the time goes in v5:
time: 146 us; the launch traced here: 145 us
  Pallas kernels  145 us (99%)
    pallas_call x1, Pallas kernels, middle(): pl.pallas_call(functools.partial(middle_kernel, blk, fch), in_specs=[vm,...  49.9 us
    pallas_call x1, Pallas kernels, back(): pl.pallas_call(functools.partial(back_kernel, nt, nb, td, plen, blk), in_...  47.5 us
    pallas_call x1, Pallas kernels, front(): pl.pallas_call(functools.partial(front_kernel, nt, nb, td, plen, chunk),...  39.1 us
    pallas_call x1, Pallas kernels, tail(): pl.pallas_call(functools.partial(tail_kernel, plen), in_specs=[vm, vm, vm...  8.03 us

profile of v5, /device:TPU:0, one launch (start us, length us, event | category | flops | bytes accessed | tf_op | source)
XLA Modules:
  0.0 145.4 jit_solution(16846189202853872410)
XLA Ops:
  0.6 39.1 %front_attend.1 = (bf16[1024,3072]{1,0:T(8,128)(2,1)}, bf16[1024,1024]{1,0:T(8,128)(2,1)}, bf16[8,5120,256]{2,1,0:T(8,128)(2,1)}, bf16[64,2048]{1,0:T(8,128)(2,1...) custom-call(s32[4,32]{1,0:T(4,128)} %bitcast.7, ...), custom_call_target="tpu_custom_call" | custom-call | tf_op jit(solution)/shard_map/front_attend/pallas_call | solution.py:331
  39.8 49.9 %middle.1 = (bf16[1024,1024]{1,0:T(8,128)(2,1)}, f32[1024,1024]{1,0:T(8,128)}, bf16[1024,1024]{1,0:T(8,128)(2,1)}) custom-call(bf16[1024]{0:T(1024)(128)(2,1)} %g_ref.4, bf16[1024]{0:T(1024)(128)(2,1)} %b_ref.3, bf16[1024,1024]{1,0:T(8,128)(2,1)} %tok_hbm.5, bf16[1024,1024]{1,0:T(8,128)(2,1)} %get-tuple-element.27.att_hbm, bf16[1024,1024]{1,0:T(8,128)(2,1)} %ct_hbm.1, ...), custom_call_target="tpu_custom_call" | custom-call | tf_op jit(solution)/shard_map/middle/pallas_call | solution.py:440
  89.7 47.5 %back_attend.1 = (bf16[1024,1024]{1,0:T(8,128)(2,1)}, bf16[256,512]{1,0:T(8,128)(2,1)}, bf16[256,256]{1,0:T(8,128)(2,1)}) custom-call(s32[4,32]{1,0:T(4,128)} %bitcast.8, s32[1,4]{1,0:T(1,128)} %len_ref.3, f32[32,512]{1,0:T(8,128)} %get-tuple-element.29.hid_ref, bf16[1024]{0:T(1024)(128)(2,1)} %g_ref.5, f32[8,2,1024]{2,1,0:T(2,128)} %get-tuple-element.30.lse_ref, ...), custom_call_target="tpu_custom_call" | custom-call | tf_op jit(solution)/shard_map/back_attend/pallas_call | solution.py:737
  137.2 8.0 %tail.1 = (f32[160,128]{1,0:T(8,128)}, f32[16,512]{1,0:T(8,128)}, f32[16,256]{1,0:T(8,128)}, bf16[1024,1024]{1,0:T(8,128)(2,1)}, f32[16,128,512]{2,1,0:T(8,128)}, /*index=5*/f32[16,512,256]{2,1,0:T(8,128)}) custom-call(bf16[10,16,128]{2,1,0:T(8,128)(2,1)} %bitcast.6, bf16[256,512]{1,0:T(8,128)(2,1)} %get-tuple-element.37.gpre_ref, ...), custom_call_target="tpu_custom_call" | custom-call | tf_op jit(solution)/shard_map/tail/pallas_call | solution.py:820

commit v6 on v5

--- a/solution.py
+++ b/solution.py
@@ -112,11 +112,11 @@
     bias = b_ref[...].astype(F).reshape(1, -1)
 
     def norm_step(i, c):
-        r = pl.ds(pl.multiple_of(i * 128, 128), 128)
+        r = pl.ds(pl.multiple_of(i * 256, 256), 256)
         normed[r, :] = layer_norm_rows(tok[r, :].astype(F), gain, bias).astype(BF)
         return c
 
-    lax.fori_loop(0, rows // 128, norm_step, 0)
+    lax.fori_loop(0, rows // 256, norm_step, 0)
     loads[2].wait()
 
     def store(j):
@@ -201,7 +201,7 @@
             cp.wait()
 
     def attend(h, c):
-        pl.when(h == 2)(send_table)
+        pl.when(h == 3)(send_table)
         pl.when(h >= 2)(lambda: p_wait(h - 2))
         buf = lax.rem(h, 2)
         part = lambda third: qkv[:, pl.ds(pl.multiple_of(third * width + h * pair, pair), pair)]

time: 146 us -> 145 us (level)
  no operation moved by 1% of the time
where the time goes in v6:
time: 145 us
  Pallas kernels  144 us (99%)
    pallas_call x1, Pallas kernels, middle(): pl.pallas_call(functools.partial(middle_kernel, blk, fch), in_specs=[vm,...  49.9 us
    pallas_call x1, Pallas kernels, back(): pl.pallas_call(functools.partial(back_kernel, nt, nb, td, plen, blk), in_...  47.5 us
    pallas_call x1, Pallas kernels, front(): pl.pallas_call(functools.partial(front_kernel, nt, nb, td, plen, chunk),...  38.5 us
    pallas_call x1, Pallas kernels, tail(): pl.pallas_call(functools.partial(tail_kernel, plen), in_specs=[vm, vm, vm...  8.03 us

profile of v6, /device:TPU:0, one launch (start us, length us, event | category | flops | bytes accessed | tf_op | source)
XLA Modules:
  0.0 144.8 jit_solution(14588698721220779475)
XLA Ops:
  0.6 38.5 %front_attend.1 = (bf16[1024,3072]{1,0:T(8,128)(2,1)}, bf16[1024,1024]{1,0:T(8,128)(2,1)}, bf16[8,5120,256]{2,1,0:T(8,128)(2,1)}, bf16[64,2048]{1,0:T(8,128)(2,1...) custom-call(s32[4,32]{1,0:T(4,128)} %bitcast.7, ...), custom_call_target="tpu_custom_call" | custom-call | tf_op jit(solution)/shard_map/front_attend/pallas_call | solution.py:331
  39.2 49.9 %middle.1 = (bf16[1024,1024]{1,0:T(8,128)(2,1)}, f32[1024,1024]{1,0:T(8,128)}, bf16[1024,1024]{1,0:T(8,128)(2,1)}) custom-call(bf16[1024]{0:T(1024)(128)(2,1)} %g_ref.4, bf16[1024]{0:T(1024)(128)(2,1)} %b_ref.3, bf16[1024,1024]{1,0:T(8,128)(2,1)} %tok_hbm.5, bf16[1024,1024]{1,0:T(8,128)(2,1)} %get-tuple-element.27.att_hbm, bf16[1024,1024]{1,0:T(8,128)(2,1)} %ct_hbm.1, ...), custom_call_target="tpu_custom_call" | custom-call | tf_op jit(solution)/shard_map/middle/pallas_call | solution.py:440
  89.1 47.5 %back_attend.1 = (bf16[1024,1024]{1,0:T(8,128)(2,1)}, bf16[256,512]{1,0:T(8,128)(2,1)}, bf16[256,256]{1,0:T(8,128)(2,1)}) custom-call(s32[4,32]{1,0:T(4,128)} %bitcast.8, s32[1,4]{1,0:T(1,128)} %len_ref.3, f32[32,512]{1,0:T(8,128)} %get-tuple-element.29.hid_ref, bf16[1024]{0:T(1024)(128)(2,1)} %g_ref.5, f32[8,2,1024]{2,1,0:T(2,128)} %get-tuple-element.30.lse_ref, ...), custom_call_target="tpu_custom_call" | custom-call | tf_op jit(solution)/shard_map/back_attend/pallas_call | solution.py:737
  136.6 8.0 %tail.1 = (f32[160,128]{1,0:T(8,128)}, f32[16,512]{1,0:T(8,128)}, f32[16,256]{1,0:T(8,128)}, bf16[1024,1024]{1,0:T(8,128)(2,1)}, f32[16,128,512]{2,1,0:T(8,128)}, /*index=5*/f32[16,512,256]{2,1,0:T(8,128)}) custom-call(bf16[10,16,128]{2,1,0:T(8,128)(2,1)} %bitcast.6, bf16[256,512]{1,0:T(8,128)(2,1)} %get-tuple-element.37.gpre_ref, ...), custom_call_target="tpu_custom_call" | custom-call | tf_op jit(solution)/shard_map/tail/pallas_call | solution.py:820

commit v7 on v6

--- a/solution.py
+++ b/solution.py
@@ -19,7 +19,7 @@
 
 
 AHEAD = 3
-PARTS = 4
+PARTS = 2
 GROUP = 4
 
 

time: 145 us -> 145 us (level)
  no operation moved by 1% of the time
where the time goes in v7:
time: 145 us
  Pallas kernels  144 us (99%)
    pallas_call x1, Pallas kernels, middle(): pl.pallas_call(functools.partial(middle_kernel, blk, fch), in_specs=[vm,...  49.9 us
    pallas_call x1, Pallas kernels, back(): pl.pallas_call(functools.partial(back_kernel, nt, nb, td, plen, blk), in_...  47.4 us
    pallas_call x1, Pallas kernels, front(): pl.pallas_call(functools.partial(front_kernel, nt, nb, td, plen, chunk),...  38.5 us
    pallas_call x1, Pallas kernels, tail(): pl.pallas_call(functools.partial(tail_kernel, plen), in_specs=[vm, vm, vm...  8.03 us

profile of v7, /device:TPU:0, one launch (start us, length us, event | category | flops | bytes accessed | tf_op | source)
XLA Modules:
  0.0 144.7 jit_solution(14135534440991010241)
XLA Ops:
  0.6 38.5 %front_attend.1 = (bf16[1024,3072]{1,0:T(8,128)(2,1)}, bf16[1024,1024]{1,0:T(8,128)(2,1)}, bf16[8,5120,256]{2,1,0:T(8,128)(2,1)}, bf16[64,2048]{1,0:T(8,128)(2,1...) custom-call(s32[4,32]{1,0:T(4,128)} %bitcast.7, ...), custom_call_target="tpu_custom_call" | custom-call | tf_op jit(solution)/shard_map/front_attend/pallas_call | solution.py:331
  39.1 49.9 %middle.1 = (bf16[1024,1024]{1,0:T(8,128)(2,1)}, f32[1024,1024]{1,0:T(8,128)}, bf16[1024,1024]{1,0:T(8,128)(2,1)}) custom-call(bf16[1024]{0:T(1024)(128)(2,1)} %g_ref.4, bf16[1024]{0:T(1024)(128)(2,1)} %b_ref.3, bf16[1024,1024]{1,0:T(8,128)(2,1)} %tok_hbm.5, bf16[1024,1024]{1,0:T(8,128)(2,1)} %get-tuple-element.27.att_hbm, bf16[1024,1024]{1,0:T(8,128)(2,1)} %ct_hbm.1, ...), custom_call_target="tpu_custom_call" | custom-call | tf_op jit(solution)/shard_map/middle/pallas_call | solution.py:440
  89.1 47.4 %back_attend.1 = (bf16[1024,1024]{1,0:T(8,128)(2,1)}, bf16[256,512]{1,0:T(8,128)(2,1)}, bf16[256,256]{1,0:T(8,128)(2,1)}) custom-call(s32[4,32]{1,0:T(4,128)} %bitcast.8, s32[1,4]{1,0:T(1,128)} %len_ref.3, f32[32,512]{1,0:T(8,128)} %get-tuple-element.29.hid_ref, bf16[1024]{0:T(1024)(128)(2,1)} %g_ref.5, f32[8,2,1024]{2,1,0:T(2,128)} %get-tuple-element.30.lse_ref, ...), custom_call_target="tpu_custom_call" | custom-call | tf_op jit(solution)/shard_map/back_attend/pallas_call | solution.py:737
  136.5 8.0 %tail.1 = (f32[160,128]{1,0:T(8,128)}, f32[16,512]{1,0:T(8,128)}, f32[16,256]{1,0:T(8,128)}, bf16[1024,1024]{1,0:T(8,128)(2,1)}, f32[16,128,512]{2,1,0:T(8,128)}, /*index=5*/f32[16,512,256]{2,1,0:T(8,128)}) custom-call(bf16[10,16,128]{2,1,0:T(8,128)(2,1)} %bitcast.6, bf16[256,512]{1,0:T(8,128)(2,1)} %get-tuple-element.37.gpre_ref, ...), custom_call_target="tpu_custom_call" | custom-call | tf_op jit(solution)/shard_map/tail/pallas_call | solution.py:820
